TPU v7x, 512 devices: a whole 4x8x8 slice. The times are simulated.
512 devices in a mesh: dp: 4 (over x), expert: 128 (over y, z, core).
Axes of the slice: x: 4, y: 8, z: 8, core: 2. Of those that a mesh axis runs over, the one named last changes fastest.
Arguments:
- tokens: bfloat16 [512, 128, 1280], P(('dp', 'expert')), may hold values from -16 to 16
- ln_gain: bfloat16 [1280], replicated, may hold values from 0.25 to 1.75
- w_router: bfloat16 [1280, 128], replicated, may hold values from -0.3354102 to 0.3354102
- w_in: bfloat16 [128, 1280, 2560], P('expert', None, 'dp'), may hold values from -0.15625 to 0.15625
- w_out: bfloat16 [128, 2560, 1280], P('expert', 'dp'), may hold values from -0.125 to 0.125
- expert_ids: int32 [512, 128], P(('dp', 'expert')), may hold values from 0 to 127
- keep: int32 [512, 128], P(('dp', 'expert')), may hold values from 0 to 1, as said below
- slots: int32 [512, 128], P(('dp', 'expert')), may hold values from 0 to 1, as said below
- logit_scale: float32 [1], replicated, may hold values from 10 to 400
Outputs:
- pair_loss: float32 [512], P(('dp', 'expert'))
- tokens_grad: bfloat16 [512, 128, 1280], P(('dp', 'expert'))
Inputs may be any that keep to these rules, and one draw needn't show every extreme that they name: `keep`: among the 128 tokens of one group, at most 2 kept tokens name any one expert; in every draw some expert receives exactly 2 kept tokens from every group. Kept tokens of one group that name one expert have distinct slots; a dropped token's slot carries no meaning.
All inputs are finite; a program needn't handle non-finite values.
Results may differ from a plain program's by a relative error of at most 0.015.
Values may be sent and summed in bfloat16 or wider, within the bound.
A program may use at most 128 MiB of HBM per device.

v0:
```python
import jax
import jax.numpy as jnp
from jax import lax
from jax.sharding import PartitionSpec as P

norm_eps = 1e-06


def activation(values):
    return jax.nn.gelu(values, approximate=False)


def layer_norm(matrix_rows, ln_gain):
    centered = matrix_rows - jnp.mean(matrix_rows, -1, keepdims=True)
    variance = jnp.mean(centered * centered, -1, keepdims=True)
    return centered * lax.rsqrt(variance + norm_eps) * ln_gain.astype(jnp.float32)


def unit_rows(pooled):
    return pooled * lax.rsqrt(jnp.sum(pooled * pooled, -1, keepdims=True) + norm_eps)


def to_experts(slot_table, matrix_rows, experts):
    packed = jnp.dot(slot_table, matrix_rows, preferred_element_type=jnp.float32).astype(
        jnp.bfloat16
    )
    packed = packed.reshape(experts, slot_table.shape[0] // experts, matrix_rows.shape[1])
    arrived = lax.all_to_all(packed, "expert", split_axis=0, concat_axis=0, tiled=True)
    return arrived.reshape(slot_table.shape[0], matrix_rows.shape[1])


def from_experts(slot_table, matrix_rows, experts):
    packed = matrix_rows.reshape(experts, slot_table.shape[0] // experts, matrix_rows.shape[1])
    arrived = lax.all_to_all(packed, "expert", split_axis=0, concat_axis=0, tiled=True)
    return jnp.einsum(
        "st,sd->td",
        slot_table,
        arrived.reshape(slot_table.shape[0], matrix_rows.shape[1]),
        preferred_element_type=jnp.float32,
    )


def over_groups(matrix_rows, step_fn):
    return step_fn(lax.all_gather(matrix_rows, "dp", axis=0, tiled=True), jnp.int32(0))


def sum_groups(partial_value, groups):
    stacked = partial_value.astype(jnp.bfloat16).reshape(
        groups, partial_value.shape[0] // groups, partial_value.shape[1]
    )
    arrived = lax.all_to_all(stacked, "dp", split_axis=0, concat_axis=0, tiled=True)
    return jnp.sum(arrived.astype(jnp.float32), 0).astype(jnp.bfloat16)


def local(tokens, ln_gain, w_router, w_in, w_out, expert_ids, keep, slots, logit_scale):
    pairs_dev, row_width, model_width = tokens.shape
    seq_len = row_width // 2
    token_count = pairs_dev * row_width
    dp_count = lax.axis_size("dp")
    experts = w_router.shape[1]
    capacity = max(2, 2 * token_count // experts)
    score_scale = logit_scale[0]
    rows_in = tokens.reshape(token_count, model_width).astype(jnp.float32)
    normed, norm_pull = jax.vjp(lambda values: layer_norm(values, ln_gain), rows_in)
    normed_b = normed.astype(jnp.bfloat16)
    routed = expert_ids.reshape(token_count)
    keep_flat = keep.reshape(token_count)
    keep_f = keep_flat.astype(jnp.float32)
    target = routed * capacity + slots.reshape(token_count)
    slot_iota = lax.broadcasted_iota(jnp.int32, (experts * capacity, token_count), 0)
    slot_table = ((slot_iota == target[None, :]) & (keep_flat[None, :] == 1)).astype(jnp.bfloat16)
    choose = (lax.broadcasted_iota(jnp.int32, (token_count, experts), 1) == routed[:, None]).astype(
        jnp.float32
    )
    logits = jnp.dot(normed_b, w_router, preferred_element_type=jnp.float32)
    expo = jnp.exp(logits)
    probs = expo / jnp.sum(expo, 1, keepdims=True)
    gate_val = jnp.sum(probs * choose, 1)
    arrived = to_experts(slot_table, normed_b, experts)
    pre_act = over_groups(
        arrived, lambda piece, start: jnp.dot(piece, w_in[0], preferred_element_type=jnp.float32)
    )
    hidden_act = activation(pre_act).astype(jnp.bfloat16)
    expert_out = sum_groups(
        jnp.dot(hidden_act, w_out[0], preferred_element_type=jnp.float32), dp_count
    )
    moe_rows = from_experts(slot_table, expert_out, experts)
    mixed_rows = rows_in + (keep_f * gate_val)[:, None] * moe_rows
    pooled = jnp.mean(mixed_rows.reshape(pairs_dev, 2, seq_len, model_width), 2)
    unit_emb, unit_pull = jax.vjp(unit_rows, pooled)
    unit_b = unit_emb.astype(jnp.bfloat16)
    everyone = lax.all_gather(unit_b, ("dp", "expert"), axis=0, tiled=True)
    pair_count = everyone.shape[0]
    images_all = everyone[:, 0]
    texts_all = everyone[:, 1]
    first_pair = lax.axis_index(("dp", "expert")) * pairs_dev
    row_scores = score_scale * jnp.einsum(
        "pd,qd->pq", unit_b[:, 0], texts_all, preferred_element_type=jnp.float32
    )
    col_scores = score_scale * jnp.einsum(
        "pd,qd->pq", unit_b[:, 1], images_all, preferred_element_type=jnp.float32
    )
    all_scores = score_scale * jnp.einsum(
        "id,jd->ij", images_all, texts_all, preferred_element_type=jnp.float32
    )
    row_tot = jax.nn.logsumexp(all_scores, 1)
    col_tot = jax.nn.logsumexp(all_scores, 0)
    row_mine = lax.dynamic_slice_in_dim(row_tot, first_pair, pairs_dev)
    col_mine = lax.dynamic_slice_in_dim(col_tot, first_pair, pairs_dev)
    column_iota = lax.broadcasted_iota(jnp.int32, (pairs_dev, pair_count), 1)
    own_column = first_pair + lax.broadcasted_iota(jnp.int32, (pairs_dev, pair_count), 0)
    diag_mask = (column_iota == own_column).astype(jnp.float32)
    diag_score = jnp.sum(row_scores * diag_mask, 1)
    pair_loss = (row_mine + col_mine - 2.0 * diag_score) * 0.5
    weight_img = (
        (jnp.exp(row_scores - row_mine[:, None]) + jnp.exp(row_scores - col_tot[None, :])) * 0.5
        - diag_mask
    ).astype(jnp.bfloat16)
    weight_txt = (
        (jnp.exp(col_scores - row_tot[None, :]) + jnp.exp(col_scores - col_mine[:, None])) * 0.5
        - diag_mask
    ).astype(jnp.bfloat16)
    d_images = score_scale * jnp.dot(weight_img, texts_all, preferred_element_type=jnp.float32)
    d_texts = score_scale * jnp.dot(weight_txt, images_all, preferred_element_type=jnp.float32)
    d_pooled = unit_pull(jnp.stack([d_images, d_texts], 1))[0]
    d_mixed = jnp.broadcast_to(
        d_pooled[:, :, None, :] / seq_len, (pairs_dev, 2, seq_len, model_width)
    ).reshape(token_count, model_width)
    d_moe = ((keep_f * gate_val)[:, None] * d_mixed).astype(jnp.bfloat16)
    d_arrived = to_experts(slot_table, d_moe, experts)

    def back_step(piece, start):
        d_act = jnp.einsum("rd,fd->rf", piece, w_out[0], preferred_element_type=jnp.float32)
        _, pull_back = jax.vjp(activation, pre_act)
        return pull_back(d_act)[0].astype(jnp.bfloat16)

    d_pre = over_groups(d_arrived, back_step)
    d_back = sum_groups(
        jnp.einsum("rf,df->rd", d_pre, w_in[0], preferred_element_type=jnp.float32), dp_count
    )
    d_normed_moe = from_experts(slot_table, d_back, experts)
    d_gate = keep_f * jnp.sum(d_mixed * moe_rows, 1) * gate_val
    d_logit = d_gate[:, None] * (choose - probs)
    router_part = jnp.dot(d_logit, w_router.astype(jnp.float32).T, precision=lax.Precision.HIGHEST)
    d_normed = d_normed_moe + router_part
    d_tokens = d_mixed + norm_pull(d_normed)[0]
    tokens_grad = (d_tokens * (128.0 * seq_len / score_scale)).astype(jnp.bfloat16)
    return (pair_loss, tokens_grad.reshape(pairs_dev, row_width, model_width))


def solution(mesh):
    in_specs = (
        P(("dp", "expert"), None, None),
        P(),
        P(),
        P("expert", None, "dp"),
        P("expert", "dp", None),
        P(("dp", "expert"), None),
        P(("dp", "expert"), None),
        P(("dp", "expert"), None),
        P(),
    )
    out_specs = (P(("dp", "expert")), P(("dp", "expert"), None, None))
    return jax.shard_map(local, mesh=mesh, in_specs=in_specs, out_specs=out_specs, check_vma=False)
```

profile of v0, /device:TPU:1, one launch (start us, length us, event | category | flops | bytes accessed | tf_op | source)
XLA Modules:
  0.0 468.4 jit_solution(9549707379720266830)
XLA Ops:
  7.2 1.2 convert_reduce_fusion
  8.4 1.2 fusion.24
  9.7 0.7 convert_element_type.85
  10.4 0.7 compare_bitcast_fusion
  11.0 0.7 add_bitcast_fusion
  11.7 1.4 convolution_convert_fusion.3
  13.1 0.2 reshape.299
  13.3 40.6 %all_to_all.30 = bf16[128,2,1280]{2,1,0:T(2,128)(2,1)S(1)} all-to-all(bf16[128,2,1280]{2,1,0:T(2,128)(2,1)S(1)} %reshape.299), channel_id=1, replica_groups=mesh['dp'=4,'expert'=128] {'expert'}, dimensions={0} | all-to-all | bytes 1310720 | tf_op jit(solution)/shard_map/all_to_all | solution.py:28
  53.9 1.1 reshape.300
  55.0 34.3 %all-gather.4.cloned.1.call-done = bf16[1024,1280]{1,0:T(8,128)(2,1)} async-done(((bf16[256,1280]{1,0:T(8,128)(2,1)}), bf16[1024,1280]{1,0:T(8,128)(2,1)}) %all-gather.4.cloned.1.call-update) | async-done | bytes 2621456 | tf_op jit(solution)/shard_map/all_gather | solution.py:44
  89.3 4.4 fusion.13
  93.8 8.1 %convolution_convert_fusion.1 = bf16[1024,1280]{1,0:T(8,128)(2,1)S(1)} fusion(bf16[1,640,1280]{2,1,0:T(8,128)(2,1)S(1)} %copy-done, f32[1024,640]{1,0:T(8,128)S(1)} %fusion.13), kind=kOutput, calls=%fused_computation.2 | convolution fusion | flops 1721630720 | bytes 6881280 | tf_op jit(solution)/shard_map/dot_general | solution.py:85
  101.8 34.4 %all_to_all.31 = bf16[4,256,1280]{2,1,0:T(8,128)(2,1)} all-to-all(bf16[4,256,1280]{2,1,0:T(8,128)(2,1)S(1)} %bitcast.117), channel_id=1, replica_groups=mesh['dp'=4,'expert'=128] {'dp'}, dimensions={0} | all-to-all | bytes 5242880 | tf_op jit(solution)/shard_map/all_to_all | solution.py:51
  136.2 2.5 reduce_sum.159
  138.7 1.1 reshape.302
  139.8 15.5 %all-to-all-start.2 = ((bf16[128,2,1280]{2,1,0:T(2,128)(2,1)}), bf16[128,2,1280]{2,1,0:T(2,128)(2,1)S(1)}, u32[]{:S(2)}, u32[]{:S(2)}) async-start(bf16[128,2,1280]{2,1,0:T(2,128)(2,1)} %reshape.302), calls=%async_computation.2 | async-start | bytes 1310720 | tf_op jit(solution)/shard_map/all_to_all | solution.py:34
  155.3 0.4 fusion.71
  155.8 21.8 %all-to-all-done.2 = bf16[128,2,1280]{2,1,0:T(2,128)(2,1)S(1)} async-done(((bf16[128,2,1280]{2,1,0:T(2,128)(2,1)}), bf16[128,2,1280]{2,1,0:T(2,128)(2,1)S(1)}, u32[]{:S(2)}, u32[]{:S(2)}) %all-to-all-start.2) | async-done | bytes 655392 | tf_op jit(solution)/shard_map/all_to_all | solution.py:34
  177.6 0.2 reshape.303
  177.9 0.3 bitcast_reduce_fusion
  178.3 0.7 fusion.53
  179.9 107.3 %all-gather.6.cloned.1.call-done = bf16[512,2,1280]{2,1,0:T(2,128)(2,1)} async-done(((bf16[1,2,1280]{2,1,0:T(2,128)(2,1)}), bf16[512,2,1280]{2,1,0:T(2,128)(2,1)}) %all-gather.6.cloned.1.call-update) | async-done | bytes 2621456 | tf_op jit(solution)/shard_map/all_gather | solution.py:92
  287.2 6.5 %fusion.70 = (bf16[512,1,1280]{2,1,0:T(2,128)(2,1)S(1)}, bf16[512,1,1280]{2,1,0:T(2,128)(2,1)S(1)}) fusion(bf16[512,2,1280]{2,1,0:T(2,128)(2,1)} %all-gather.6.cloned.1.call-done), kind=kLoop, calls=%fused_computation.121 | loop fusion | bytes 5242880 | tf_op jit(solution)/shard_map/slice | solution.py:95
  293.7 0.4 fusion.55
  294.2 0.5 fusion.54
  294.6 1.0 fusion.68
  295.6 0.4 exponential_reduce_fusion
  296.0 0.6 dynamic_slice.6
  296.6 1.3 fusion.56
  297.9 0.3 convolution_reduce_fusion.1
  298.2 0.6 dynamic_slice.7
  298.8 0.6 fusion.57
  299.5 0.3 convolution_reduce_fusion
  300.2 0.3 convolution_convert_fusion.2
  300.5 0.2 reshape.307
  300.8 31.5 %all_to_all.32 = bf16[128,2,1280]{2,1,0:T(2,128)(2,1)S(1)} all-to-all(bf16[128,2,1280]{2,1,0:T(2,128)(2,1)S(1)} %reshape.307), channel_id=1, replica_groups=mesh['dp'=4,'expert'=128] {'expert'}, dimensions={0} | all-to-all | bytes 1310720 | tf_op jit(solution)/shard_map/all_to_all | solution.py:28
  332.3 1.1 reshape.308
  333.4 33.9 %all-gather.8.cloned.1.call-done = bf16[1024,1280]{1,0:T(8,128)(2,1)} async-done(((bf16[256,1280]{1,0:T(8,128)(2,1)}), bf16[1024,1280]{1,0:T(8,128)(2,1)}) %all-gather.8.cloned.1.call-update) | async-done | bytes 2621456 | tf_op jit(solution)/shard_map/all_gather | solution.py:44
  367.3 13.0 %convolution_convert_fusion = bf16[1024,1280]{1,0:T(8,128)(2,1)} fusion(bf16[1,1280,640]{2,1,0:T(8,128)(2,1)} %param.12, f32[1024,640]{1,0:T(8,128)} %copy-done.6, bf16[1024,1280]{1,0:T(8,128)(2,1)} %all-gather.8.cloned.1.call-done, bf16[1,640,1280]{2,1,0:T(8,128)(2,1)S(1)} %copy-done), kind=kOutput, calls=%fused_computation.1 | convolution fusion | flops 3403939840 | bytes 11141120 | tf_op jit(solution)/shard_map/rf,df->rd/dot_general | solution.py:139
  380.3 35.5 %all_to_all.33 = bf16[4,256,1280]{2,1,0:T(8,128)(2,1)} all-to-all(bf16[4,256,1280]{2,1,0:T(8,128)(2,1)} %bitcast.116), channel_id=1, replica_groups=mesh['dp'=4,'expert'=128] {'dp'}, dimensions={0} | all-to-all | bytes 5242880 | tf_op jit(solution)/shard_map/all_to_all | solution.py:51
  415.9 2.4 reduce_sum.167
  418.3 1.1 reshape.310
  419.4 15.7 %all-to-all-start.5 = ((bf16[128,2,1280]{2,1,0:T(2,128)(2,1)}), bf16[128,2,1280]{2,1,0:T(2,128)(2,1)S(1)}, u32[]{:S(2)}, u32[]{:S(2)}) async-start(bf16[128,2,1280]{2,1,0:T(2,128)(2,1)} %reshape.310), calls=%async_computation.5 | async-start | bytes 1310720 | tf_op jit(solution)/shard_map/all_to_all | solution.py:34
  437.0 20.4 %all-to-all-done.5 = bf16[128,2,1280]{2,1,0:T(2,128)(2,1)S(1)} async-done(((bf16[128,2,1280]{2,1,0:T(2,128)(2,1)}), bf16[128,2,1280]{2,1,0:T(2,128)(2,1)S(1)}, u32[]{:S(2)}, u32[]{:S(2)}) %all-to-all-start.5) | async-done | bytes 655392 | tf_op jit(solution)/shard_map/all_to_all | solution.py:34
  457.7 0.3 fusion.33
  458.0 1.6 fusion.27
  459.6 0.3 fusion.69
  459.9 0.9 fusion.31
  (42 shorter events, 1.3 us)
Async XLA Ops:
  7.2 86.6 %copy-start = (bf16[1,640,1280]{2,1,0:T(8,128)(2,1)S(1)}, bf16[1,640,1280]{2,1,0:T(8,128)(2,1)}, u32[]{:S(2)}) copy-start(bf16[1,640,1280]{2,1,0:T(8,128)(2,1)} %param.13) | copy-start | bytes 4915204
  7.2 82.1 %all-gather.4.cloned.1.call-start = ((), (), s32[]{:S(2)}) async-start(), calls=%async_computation.6 | async-start | bytes 3276800 | tf_op jit(solution)/shard_map/all_gather | solution.py:44
  93.7 8.1 %copy-start.6 = (f32[1024,640]{1,0:T(8,128)}, f32[1024,640]{1,0:T(8,128)S(1)}, u32[]{:S(2)}) copy-start(f32[1024,640]{1,0:T(8,128)S(1)} %fusion.13) | copy-start | bytes 7864324
  136.2 19.1 %copy-start.1 = (bf16[1,128,1280]{2,1,0:T(8,128)(2,1)S(1)}, bf16[1,128,1280]{2,1,0:T(8,128)(2,1)}, u32[]{:S(2)}) copy-start(bf16[1,128,1280]{2,1,0:T(8,128)(2,1)} %param.9) | copy-start | bytes 983044
  136.2 19.1 %copy-start.2 = (bf16[1280,128]{1,0:T(8,128)(2,1)S(1)}, bf16[1280,128]{1,0:T(8,128)(2,1)}, u32[]{:S(2)}) copy-start(bf16[1280,128]{1,0:T(8,128)(2,1)} %param.11) | copy-start | bytes 983044
  138.7 17.0 %copy-start.4 = (s32[1,128]{1,0:T(1,128)S(1)}, s32[1,128]{1,0:T(1,128)}, u32[]{:S(2)}) copy-start(s32[1,128]{1,0:T(1,128)} %param.14) | copy-start | bytes 1540
  138.7 17.1 %copy-start.5 = (s32[1,128]{1,0:T(1,128)S(1)}, s32[1,128]{1,0:T(1,128)}, u32[]{:S(2)}) copy-start(s32[1,128]{1,0:T(1,128)} %param.15) | copy-start | bytes 1540
  139.8 37.8 %all-to-all-start.2 = ((bf16[128,2,1280]{2,1,0:T(2,128)(2,1)}), bf16[128,2,1280]{2,1,0:T(2,128)(2,1)S(1)}, u32[]{:S(2)}, u32[]{:S(2)}) async-start(bf16[128,2,1280]{2,1,0:T(2,128)(2,1)} %reshape.302), calls=%async_computation.2 | async-start | bytes 1310720 | tf_op jit(solution)/shard_map/all_to_all | solution.py:34
  155.3 132.0 %all-gather.6.cloned.1.call-start = ((), (), s32[]{:S(2)}) async-start(), calls=%async_computation.7 | async-start | bytes 2626560 | tf_op jit(solution)/shard_map/all_gather | solution.py:92
  179.0 188.3 %all-gather.8.cloned.1.call-start = ((), (), s32[]{:S(2)}) async-start(), calls=%async_computation.8 | async-start | bytes 3276800 | tf_op jit(solution)/shard_map/all_gather | solution.py:44
  179.9 113.8 %copy-start.3 = (bf16[1,2,1280]{2,1,0:T(2,128)(2,1)S(1)}, bf16[1,2,1280]{2,1,0:T(2,128)(2,1)}, u32[]{:S(2)}) copy-start(bf16[1,2,1280]{2,1,0:T(2,128)(2,1)} %fusion.53) | copy-start | bytes 15364
  419.4 38.0 %all-to-all-start.5 = ((bf16[128,2,1280]{2,1,0:T(2,128)(2,1)}), bf16[128,2,1280]{2,1,0:T(2,128)(2,1)S(1)}, u32[]{:S(2)}, u32[]{:S(2)}) async-start(bf16[128,2,1280]{2,1,0:T(2,128)(2,1)} %reshape.310), calls=%async_computation.5 | async-start | bytes 1310720 | tf_op jit(solution)/shard_map/all_to_all | solution.py:34
Sparse Core Ops, SparseCore 0:
  55.1 34.1 all-gather.3
  179.1 108.0 all-gather.5
  333.6 33.7 all-gather.7
where the time goes:
time: 469 us; the launch traced here: 468 us
  waiting for transfers between devices  218 us (46%)
  blocking collectives  142 us (30%)
  matrix products  32.3 us (7%)
  starting transfers between devices  31.4 us (7%)
  between operations  17.8 us (4%)
  other arithmetic  14.2 us (3%)
  local copies, waits for them, and re-layouts  13.1 us (3%)
    all_gather x1, waiting for transfers between devices, local(): everyone = lax.all_gather(unit_b, ('dp', 'expert'), axis=0, tiled=True)  107 us
    all_to_all x2, blocking collectives, to_experts(): lax.all_to_all(packed, 'expert', split_axis=0, concat_axis=0, tiled=True)  72.1 us
    all_to_all x2, blocking collectives, sum_groups(): lax.all_to_all(stacked, 'dp', split_axis=0, concat_axis=0, tiled=True)  69.9 us
    all_gather x2, waiting for transfers between devices, over_groups(): lax.all_gather(matrix_rows, 'dp', axis=0, tiled=True)  68.2 us
    all_to_all x2, waiting for transfers between devices, from_experts(): lax.all_to_all(packed, 'expert', split_axis=0, concat_axis=0, tiled=True)  42.2 us
    all_to_all x2, starting transfers between devices, from_experts(): lax.all_to_all(packed, 'expert', split_axis=0, concat_axis=0, tiled=True)  31.1 us
    dot_general x1, matrix products, local(): jnp.einsum('rf,df->rd', d_pre, w_in[0], preferred_element_type=jnp.float32)  13 us
  transfers between devices with their start and end apart: 5, of which 5 were waited for; matrix products, arithmetic and copies ran while one was open for 0% of the time, Pallas kernels for 0%

commit v1 on v0

--- a/solution.py
+++ b/solution.py
@@ -1,13 +1,26 @@
+import functools
+
 import jax
 import jax.numpy as jnp
 from jax import lax
+from jax.experimental import pallas as pl
+from jax.experimental.pallas import tpu as pltpu
 from jax.sharding import PartitionSpec as P
 
+MESH = pl.DeviceIdType.MESH
 norm_eps = 1e-06
+CHUNKS = 5
+CORES = 2
+SLOTS = 2
 
 
 def activation(values):
-    return jax.nn.gelu(values, approximate=False)
+    return 0.5 * values * (1.0 + lax.erf(values * (0.5**0.5)))
+
+
+def activation_slope(values):
+    bell = jnp.exp(-0.5 * values * values) * 0.3989422804014327
+    return 0.5 * (1.0 + lax.erf(values * (0.5**0.5))) + values * bell
 
 
 def layer_norm(matrix_rows, ln_gain):
@@ -20,36 +33,425 @@
     return pooled * lax.rsqrt(jnp.sum(pooled * pooled, -1, keepdims=True) + norm_eps)
 
 
-def to_experts(slot_table, matrix_rows, experts):
-    packed = jnp.dot(slot_table, matrix_rows, preferred_element_type=jnp.float32).astype(
-        jnp.bfloat16
+def chip_sides(experts):
+    chips = experts // CORES
+    side = 1
+    while side * side < chips:
+        side *= 2
+    return side, chips // side
+
+
+def near_first(count):
+    offsets = []
+    for step in range(1, count // 2 + 1):
+        offsets.append(step)
+        if count - step != step:
+            offsets.append(count - step)
+    return offsets
+
+
+def send(src, dst, send_sem, recv_sem, device):
+    pltpu.make_async_remote_copy(
+        src_ref=src,
+        dst_ref=dst,
+        send_sem=send_sem,
+        recv_sem=recv_sem,
+        device_id=device,
+        device_id_type=MESH,
+    ).start()
+
+
+def drain(ref, sem):
+    pltpu.make_async_copy(ref, ref, sem).wait()
+
+
+def greet(peers):
+    barrier = pltpu.get_barrier_semaphore()
+    for peer in peers:
+        pl.semaphore_signal(barrier, inc=1, device_id=peer, device_id_type=MESH)
+    pl.semaphore_wait(barrier, len(peers))
+
+
+def from_slots(slot_table, matrix_rows):
+    return jnp.einsum("st,sd->td", slot_table, matrix_rows, preferred_element_type=jnp.float32)
+
+
+def moe_kernel(backward, ny, nz, *refs):
+    if backward:
+        src, w_in, w_out, pre, out = refs[:5]
+        acc, slope = refs[-2:]
+    else:
+        src, w_in, w_out, out, pre = refs[:5]
+        acc = pre
+    ybuf, zsend, zbuf, xl, xr, xo, so, sr, sl, fl, fr, zs, zr, ys, yr = refs[5:20]
+    ol, orr, keep_r, keep_l, own, hid, perm = refs[20:27]
+    s_y, r_y, s_z, r_z, s_x, r_x, s_o, r_o = refs[27:35]
+    s_p, r_p, s_q, r_q, s_zr, r_zr, s_yr, r_yr = refs[35:43]
+    n, rows, width = ybuf.shape
+    half = rows // 2
+    top, low = pl.ds(0, half), pl.ds(half, half)
+    nzc = nz * CORES
+    yb, zb = nzc * SLOTS, ny * SLOTS
+    dpn = lax.axis_size("dp")
+    x = lax.axis_index("dp")
+    rank = lax.axis_index("expert")
+    y, zc = lax.div(rank, nzc), lax.rem(rank, nzc)
+    right, left = (lax.rem(x + 1, dpn), rank), (lax.rem(x + dpn - 1, dpn), rank)
+
+    def y_block(index):
+        return pl.ds(pl.multiple_of(index * yb, yb), yb)
+
+    def z_block(index):
+        return pl.ds(pl.multiple_of(index * zb, zb), zb)
+
+    y_peers = [lax.rem(y + k, ny) for k in near_first(ny)]
+    z_peers = [lax.rem(zc + k, nzc) for k in near_first(nzc)]
+
+    greet(
+        [(x, peer * nzc + zc) for peer in y_peers]
+        + [(x, y * nzc + peer) for peer in z_peers]
+        + [right, left]
     )
-    packed = packed.reshape(experts, slot_table.shape[0] // experts, matrix_rows.shape[1])
-    arrived = lax.all_to_all(packed, "expert", split_axis=0, concat_axis=0, tiled=True)
-    return arrived.reshape(slot_table.shape[0], matrix_rows.shape[1])
-
-
-def from_experts(slot_table, matrix_rows, experts):
-    packed = matrix_rows.reshape(experts, slot_table.shape[0] // experts, matrix_rows.shape[1])
-    arrived = lax.all_to_all(packed, "expert", split_axis=0, concat_axis=0, tiled=True)
-    return jnp.einsum(
-        "st,sd->td",
-        slot_table,
-        arrived.reshape(slot_table.shape[0], matrix_rows.shape[1]),
-        preferred_element_type=jnp.float32,
-    )
-
-
-def over_groups(matrix_rows, step_fn):
-    return step_fn(lax.all_gather(matrix_rows, "dp", axis=0, tiled=True), jnp.int32(0))
-
-
-def sum_groups(partial_value, groups):
-    stacked = partial_value.astype(jnp.bfloat16).reshape(
-        groups, partial_value.shape[0] // groups, partial_value.shape[1]
-    )
-    arrived = lax.all_to_all(stacked, "dp", split_axis=0, concat_axis=0, tiled=True)
-    return jnp.sum(arrived.astype(jnp.float32), 0).astype(jnp.bfloat16)
+
+    for t in range(n):
+        for peer in y_peers:
+            send(
+                src.at[y_block(peer), pl.ds(t * width, width)],
+                ybuf.at[t, y_block(y)],
+                s_y.at[t],
+                r_y.at[t],
+                (x, peer * nzc + zc),
+            )
+
+    place = lax.broadcasted_iota(jnp.int32, (rows, rows), 0)
+    col = lax.broadcasted_iota(jnp.int32, (rows, rows), 1)
+    for k, (fine, coarse) in enumerate(((zb, yb), (yb, zb))):
+        within = place & (fine - 1)
+        want = (within >> 1) * coarse + (place >> (fine.bit_length() - 1)) * SLOTS + (within & 1)
+        perm[k] = (col == want).astype(jnp.float32).astype(jnp.bfloat16)
+
+    slab = 16
+
+    def by_slab(step):
+        def body(i, carry):
+            at = pl.ds(pl.multiple_of(i * slab, slab), slab)
+            for b in range(4):
+                step(b, at)
+            return carry
+
+        lax.fori_loop(0, rows // slab, body, 0)
+
+    if backward:
+
+        def slope_step(b, at):
+            slope[b, at, :] = activation_slope(pre[b, at, :])
+
+        by_slab(slope_step)
+
+    def cols(t):
+        return slice(t * width, (t + 1) * width)
+
+    def product_in(block, t):
+        if backward:
+            return lax.dot_general(
+                block, w_out[:, cols(t)], (((1,), (1,)), ((), ())), preferred_element_type=jnp.float32
+            )
+        return jnp.dot(block, w_in[cols(t), :], preferred_element_type=jnp.float32)
+
+    def product_out(b, t):
+        if backward:
+            return lax.dot_general(
+                hid[b], w_in[cols(t), :], (((1,), (1,)), ((), ())), preferred_element_type=jnp.float32
+            )
+        return jnp.dot(hid[b], w_out[:, cols(t)], preferred_element_type=jnp.float32)
+
+    def stage_z(t):
+        ybuf[t, y_block(y), :] = src[y_block(y), cols(t)]
+        drain(ybuf.at[t, pl.ds(0, rows - yb)], r_y.at[t])
+        zsend[t] = jnp.dot(perm[0], ybuf[t], preferred_element_type=jnp.float32).astype(jnp.bfloat16)
+        for peer in z_peers:
+            send(
+                zsend.at[t, z_block(peer)],
+                zbuf.at[t, z_block(zc)],
+                s_z.at[t],
+                r_z.at[t],
+                (x, y * nzc + peer),
+            )
+        zbuf[t, z_block(zc), :] = zsend[t, z_block(zc), :]
+
+    def stage_x(t):
+        drain(zbuf.at[t, pl.ds(0, rows - zb)], r_z.at[t])
+        send(zbuf.at[t], xl.at[t], s_x.at[t, 0], r_x.at[t, 0], right)
+        send(zbuf.at[t], xr.at[t], s_x.at[t, 1], r_x.at[t, 1], left)
+
+    def stage_forward(t):
+        drain(xl.at[t], r_x.at[t, 0])
+        send(xl.at[t, top], xo.at[t, top], s_o.at[t, 0], r_o.at[t, 0], right)
+        drain(xr.at[t], r_x.at[t, 1])
+        send(xr.at[t, low], xo.at[t, low], s_o.at[t, 1], r_o.at[t, 1], left)
+
+    def stage_in(t):
+        drain(xo.at[t, top], r_o.at[t, 0])
+        drain(xo.at[t, low], r_o.at[t, 1])
+        for b, block in enumerate((zbuf, xl, xr, xo)):
+            part = product_in(block[t], t)
+            acc[b] = part if t == 0 else acc[b] + part
+
+    for t in range(n + 3):
+        if t < n:
+            stage_z(t)
+        if 0 <= t - 1 < n:
+            stage_x(t - 1)
+        if 0 <= t - 2 < n:
+            stage_forward(t - 2)
+        if 0 <= t - 3 < n:
+            stage_in(t - 3)
+
+    def hidden_step(b, at):
+        values = acc[b, at, :]
+        values = values * slope[b, at, :] if backward else activation(values)
+        hid[b, at, :] = values.astype(jnp.bfloat16)
+
+    by_slab(hidden_step)
+
+    def stage_out(t):
+        so[t] = product_out(3, t).astype(jnp.bfloat16)
+        send(so.at[t, top], ol.at[t], s_p.at[t, 0], r_p.at[t, 0], right)
+        send(so.at[t, low], orr.at[t], s_p.at[t, 1], r_p.at[t, 1], left)
+        part = product_out(2, t)
+        sr[t, half:, :] = part[half:].astype(jnp.bfloat16)
+        send(sr.at[t, low], fl.at[t, low], s_q.at[t, 0], r_q.at[t, 0], right)
+        keep_r[t] = part[:half]
+        part = product_out(1, t)
+        sl[t, :half, :] = part[:half].astype(jnp.bfloat16)
+        send(sl.at[t, top], fr.at[t, top], s_q.at[t, 1], r_q.at[t, 1], left)
+        keep_l[t] = part[half:]
+        own[t] = product_out(0, t)
+
+    def stage_add(t):
+        drain(ol.at[t], r_p.at[t, 0])
+        sr[t, :half, :] = (keep_r[t] + ol[t].astype(jnp.float32)).astype(jnp.bfloat16)
+        send(sr.at[t, top], fl.at[t, top], s_q.at[t, 0], r_q.at[t, 0], right)
+        drain(orr.at[t], r_p.at[t, 1])
+        sl[t, half:, :] = (keep_l[t] + orr[t].astype(jnp.float32)).astype(jnp.bfloat16)
+        send(sl.at[t, low], fr.at[t, low], s_q.at[t, 1], r_q.at[t, 1], left)
+
+    def stage_back_z(t):
+        drain(fl.at[t], r_q.at[t, 0])
+        drain(fr.at[t], r_q.at[t, 1])
+        total = own[t] + fl[t].astype(jnp.float32) + fr[t].astype(jnp.float32)
+        zs[t] = total.astype(jnp.bfloat16)
+        for peer in z_peers:
+            send(
+                zs.at[t, z_block(peer)],
+                zr.at[t, z_block(zc)],
+                s_zr.at[t],
+                r_zr.at[t],
+                (x, y * nzc + peer),
+            )
+        zr[t, z_block(zc), :] = zs[t, z_block(zc), :]
+
+    def stage_back_y(t):
+        drain(zr.at[t, pl.ds(0, rows - zb)], r_zr.at[t])
+        ys[t] = jnp.dot(perm[1], zr[t], preferred_element_type=jnp.float32).astype(jnp.bfloat16)
+        for peer in y_peers:
+            send(
+                ys.at[t, y_block(peer)],
+                yr.at[t, y_block(y)],
+                s_yr.at[t],
+                r_yr.at[t],
+                (x, peer * nzc + zc),
+            )
+        yr[t, y_block(y), :] = ys[t, y_block(y), :]
+
+    def stage_store(t):
+        drain(yr.at[t, pl.ds(0, rows - yb)], r_yr.at[t])
+        out[:, cols(t)] = yr[t]
+
+    for t in range(n + 4):
+        if t < n:
+            stage_out(t)
+        if 0 <= t - 1 < n:
+            stage_add(t - 1)
+        if 0 <= t - 2 < n:
+            stage_back_z(t - 2)
+        if 0 <= t - 3 < n:
+            stage_back_y(t - 3)
+        if 0 <= t - 4 < n:
+            stage_store(t - 4)
+
+    for t in range(n):
+        drain(ybuf.at[t, pl.ds(0, rows - yb)], s_y.at[t])
+        drain(zsend.at[t, pl.ds(0, rows - zb)], s_z.at[t])
+        drain(zs.at[t, pl.ds(0, rows - zb)], s_zr.at[t])
+        drain(ys.at[t, pl.ds(0, rows - yb)], s_yr.at[t])
+        for way in range(2):
+            drain(zbuf.at[t], s_x.at[t, way])
+            drain(xo.at[t, top], s_o.at[t, way])
+            drain(so.at[t, top], s_p.at[t, way])
+            drain(sr.at[t], s_q.at[t, way])
+
+
+def moe_call(backward, experts, packed, w_in, w_out, pre=None):
+    ny, nz = chip_sides(experts)
+    rows, model_width = packed.shape
+    hidden = w_in.shape[1]
+    n, width = CHUNKS, model_width // CHUNKS
+    half = rows // 2
+    bf16, f32 = jnp.bfloat16, jnp.float32
+    vmem = pl.BlockSpec(memory_space=pltpu.VMEM)
+    dma = pltpu.SemaphoreType.DMA
+    scratch = [pltpu.VMEM((n, rows, width), bf16) for _ in range(15)]
+    scratch += [pltpu.VMEM((n, half, width), bf16) for _ in range(2)]
+    scratch += [pltpu.VMEM((n, half, width), f32) for _ in range(2)]
+    scratch += [pltpu.VMEM((n, rows, width), f32)]
+    scratch += [pltpu.VMEM((4, rows, hidden), bf16), pltpu.VMEM((2, rows, rows), bf16)]
+    scratch += [dma((n,)) for _ in range(4)] + [dma((n, 2)) for _ in range(8)] + [dma((n,)) for _ in range(4)]
+    if backward:
+        scratch += [pltpu.VMEM((4, rows, hidden), f32) for _ in range(2)]
+    out_shape = [jax.ShapeDtypeStruct((rows, model_width), bf16)]
+    operands = [packed, w_in, w_out]
+    if backward:
+        operands.append(pre)
+    else:
+        out_shape.append(jax.ShapeDtypeStruct((4, rows, hidden), f32))
+    return pl.pallas_call(
+        functools.partial(moe_kernel, backward, ny, nz),
+        out_shape=out_shape,
+        in_specs=[vmem] * len(operands),
+        out_specs=[vmem] * len(out_shape),
+        scratch_shapes=scratch,
+        name="moe_back" if backward else "moe_fore",
+        compiler_params=pltpu.CompilerParams(
+            collective_id=1 if backward else 0,
+            has_side_effects=True,
+            vmem_limit_bytes=56 * 1024 * 1024,
+        ),
+    )(*operands)
+
+
+def gather_kernel(ny, nz, u, out, near, block, half_block, held, s_n, r_n, s_a, r_a, s_b, r_b, s_c, r_c):
+    dpn = lax.axis_size("dp")
+    x = lax.axis_index("dp")
+    rank = lax.axis_index("expert")
+    c = lax.rem(rank, CORES)
+    z = lax.rem(lax.div(rank, CORES), nz)
+    y = lax.div(rank, CORES * nz)
+    side = ny
+    near_count = dpn * CORES
+    own_near = x * CORES + c
+    first = z * (1 - c) + y * c
+    second = y * (1 - c) + z * c
+
+    def at_rank(first_at, second_at):
+        y_at = second_at * (1 - c) + first_at * c
+        z_at = first_at * (1 - c) + second_at * c
+        return (x, (y_at * nz + z_at) * CORES + c)
+
+    near_peers = []
+    for k in range(1, near_count):
+        peer = lax.rem(own_near + k, near_count)
+        near_peers.append((lax.div(peer, CORES), (y * nz + z) * CORES + lax.rem(peer, CORES)))
+    a_peers = [at_rank(lax.rem(first + k, side), second) for k in near_first(side)]
+    right = at_rank(first, lax.rem(second + 1, side))
+    left = at_rank(first, lax.rem(second + side - 1, side))
+    sibling = (x, rank + 1 - 2 * c)
+    ring = [right] if side == 2 else [right, left]
+    greet(near_peers + a_peers + ring)
+
+    for peer in near_peers:
+        send(u, near.at[own_near], s_n.at[0], r_n.at[0], peer)
+    near[own_near] = u[...]
+    drain(near.at[pl.ds(0, near_count - 1)], r_n.at[0])
+    for k in range(near_count):
+        for m in range(2):
+            block[m * near_count + k : m * near_count + k + 1, :] = near[k, m : m + 1, :]
+    half_width = half_block.shape[1]
+    half_block[...] = jnp.where(c == 0, block[:, :half_width], block[:, half_width:]).astype(jnp.bfloat16)
+    held[c, second, first] = half_block[...]
+    for peer in a_peers:
+        send(half_block, held.at[c, second, first], s_a.at[0], r_a.at[0], peer)
+    drain(held.at[c, second, pl.ds(0, side - 1)], r_a.at[0])
+
+    def share(slab, k):
+        send(slab, slab, s_c.at[k], r_c.at[k], sibling)
+
+    share(held.at[c, second], 0)
+    full = side // 2 - 1
+    for i in range(full):
+        r_slab = held.at[c, lax.rem(second + side - i, side)]
+        l_slab = held.at[c, lax.rem(second + i, side)]
+        send(r_slab, r_slab, s_b.at[i, 0], r_b.at[i, 0], right)
+        send(l_slab, l_slab, s_b.at[i, 1], r_b.at[i, 1], left)
+        for way, got in enumerate((second + side - i - 1, second + i + 1)):
+            slab = held.at[c, lax.rem(got, side)]
+            drain(slab, r_b.at[i, way])
+            share(slab, 1 + 2 * i + way)
+    parts = (pl.ds(0, side // 2), pl.ds(side // 2, side // 2))
+    r_slab = held.at[c, lax.rem(second + side - full, side), parts[0]]
+    l_slab = held.at[c, lax.rem(second + full, side), parts[1]]
+    send(r_slab, r_slab, s_b.at[full, 0], r_b.at[full, 0], right)
+    send(l_slab, l_slab, s_b.at[full, 1], r_b.at[full, 1], left)
+    for way in range(2):
+        slab = held.at[c, lax.rem(second + side // 2, side), parts[way]]
+        drain(slab, r_b.at[full, way])
+        share(slab, 1 + 2 * full + way)
+
+    for k in range(1 + 2 * full):
+        drain(held.at[0, 0], r_c.at[k])
+    for way in range(2):
+        drain(held.at[0, 0, parts[way]], r_c.at[1 + 2 * full + way])
+    for b in range(side):
+        for a in range(side):
+            out[b * nz + a, :, :half_width] = held[0, b, a]
+            out[a * nz + b, :, half_width:] = held[1, b, a]
+
+    drain(near.at[pl.ds(0, near_count - 1)], s_n.at[0])
+    drain(held.at[c, second, pl.ds(0, side - 1)], s_a.at[0])
+    for i in range(full):
+        for way in range(2):
+            drain(held.at[0, 0], s_b.at[i, way])
+    for way in range(2):
+        drain(held.at[0, 0, parts[way]], s_b.at[full, way])
+    for k in range(1 + 2 * full):
+        drain(held.at[0, 0], s_c.at[k])
+    for way in range(2):
+        drain(held.at[0, 0, parts[way]], s_c.at[1 + 2 * full + way])
+
+
+def gather_call(experts, u):
+    ny, nz = chip_sides(experts)
+    side = ny
+    model_width = u.shape[1]
+    near_count = lax.axis_size("dp") * CORES
+    rows = 2 * near_count
+    steps = side // 2
+    dma = pltpu.SemaphoreType.DMA
+    vmem = pl.BlockSpec(memory_space=pltpu.VMEM)
+    return pl.pallas_call(
+        functools.partial(gather_kernel, ny, nz),
+        out_shape=jax.ShapeDtypeStruct((ny * nz, rows, model_width), jnp.bfloat16),
+        in_specs=[vmem],
+        out_specs=vmem,
+        scratch_shapes=[
+            pltpu.VMEM((near_count, 2, model_width), jnp.float32),
+            pltpu.VMEM((rows, model_width), jnp.float32),
+            pltpu.VMEM((rows, model_width // 2), jnp.bfloat16),
+            pltpu.VMEM((2, side, side, rows, model_width // 2), jnp.bfloat16),
+            dma((1,)),
+            dma((1,)),
+            dma((1,)),
+            dma((1,)),
+            dma((steps, 2)),
+            dma((steps, 2)),
+            dma((2 * steps + 1,)),
+            dma((2 * steps + 1,)),
+        ],
+        name="gather_units",
+        compiler_params=pltpu.CompilerParams(
+            collective_id=2, has_side_effects=True, vmem_limit_bytes=48 * 1024 * 1024
+        ),
+    )(u)
 
 
 def local(tokens, ln_gain, w_router, w_in, w_out, expert_ids, keep, slots, logit_scale):
@@ -76,24 +478,20 @@
     expo = jnp.exp(logits)
     probs = expo / jnp.sum(expo, 1, keepdims=True)
     gate_val = jnp.sum(probs * choose, 1)
-    arrived = to_experts(slot_table, normed_b, experts)
-    pre_act = over_groups(
-        arrived, lambda piece, start: jnp.dot(piece, w_in[0], preferred_element_type=jnp.float32)
-    )
-    hidden_act = activation(pre_act).astype(jnp.bfloat16)
-    expert_out = sum_groups(
-        jnp.dot(hidden_act, w_out[0], preferred_element_type=jnp.float32), dp_count
-    )
-    moe_rows = from_experts(slot_table, expert_out, experts)
+    packed = jnp.dot(slot_table, normed_b, preferred_element_type=jnp.float32).astype(jnp.bfloat16)
+    expert_out, pre_act = moe_call(False, experts, packed, w_in[0], w_out[0])
+    moe_rows = from_slots(slot_table, expert_out)
     mixed_rows = rows_in + (keep_f * gate_val)[:, None] * moe_rows
     pooled = jnp.mean(mixed_rows.reshape(pairs_dev, 2, seq_len, model_width), 2)
     unit_emb, unit_pull = jax.vjp(unit_rows, pooled)
     unit_b = unit_emb.astype(jnp.bfloat16)
-    everyone = lax.all_gather(unit_b, ("dp", "expert"), axis=0, tiled=True)
-    pair_count = everyone.shape[0]
-    images_all = everyone[:, 0]
-    texts_all = everyone[:, 1]
-    first_pair = lax.axis_index(("dp", "expert")) * pairs_dev
+    everyone = gather_call(experts, unit_b[0].astype(jnp.float32))
+    near_count = dp_count * CORES
+    images_all = everyone[:, :near_count].reshape(-1, model_width)
+    texts_all = everyone[:, near_count:].reshape(-1, model_width)
+    pair_count = images_all.shape[0]
+    rank = lax.axis_index("expert")
+    first_pair = (rank // CORES) * near_count + lax.axis_index("dp") * CORES + rank % CORES
     row_scores = score_scale * jnp.einsum(
         "pd,qd->pq", unit_b[:, 0], texts_all, preferred_element_type=jnp.float32
     )
@@ -127,18 +525,9 @@
         d_pooled[:, :, None, :] / seq_len, (pairs_dev, 2, seq_len, model_width)
     ).reshape(token_count, model_width)
     d_moe = ((keep_f * gate_val)[:, None] * d_mixed).astype(jnp.bfloat16)
-    d_arrived = to_experts(slot_table, d_moe, experts)
-
-    def back_step(piece, start):
-        d_act = jnp.einsum("rd,fd->rf", piece, w_out[0], preferred_element_type=jnp.float32)
-        _, pull_back = jax.vjp(activation, pre_act)
-        return pull_back(d_act)[0].astype(jnp.bfloat16)
-
-    d_pre = over_groups(d_arrived, back_step)
-    d_back = sum_groups(
-        jnp.einsum("rf,df->rd", d_pre, w_in[0], preferred_element_type=jnp.float32), dp_count
-    )
-    d_normed_moe = from_experts(slot_table, d_back, experts)
+    d_packed = jnp.dot(slot_table, d_moe, preferred_element_type=jnp.float32).astype(jnp.bfloat16)
+    d_back = moe_call(True, experts, d_packed, w_in[0], w_out[0], pre_act)[0]
+    d_normed_moe = from_slots(slot_table, d_back)
     d_gate = keep_f * jnp.sum(d_mixed * moe_rows, 1) * gate_val
     d_logit = d_gate[:, None] * (choose - probs)
     router_part = jnp.dot(d_logit, w_router.astype(jnp.float32).T, precision=lax.Precision.HIGHEST)

time: 469 us -> 250 us (0.53)
  Pallas kernels: 0 us -> 226 us
  waiting for transfers between devices: 218 us -> 0 us
  blocking collectives: 142 us -> 0 us
  starting transfers between devices: 31.4 us -> 0 us
  matrix products: 32.3 us -> 10.5 us
  between operations: 17.8 us -> 4.58 us
  local copies, waits for them, and re-layouts: 13.1 us -> 1.24 us
  other arithmetic: 14.2 us -> 7.37 us
    pallas_call x0 -> x3, Pallas kernels: none -> 226 us  [the longest x2 190 us: moe_call(): pl.pallas_call(functools.partial(moe_kernel, backward, ny, nz), out_shape...]
    all_gather x3 -> x0, waiting for transfers between devices: 175 us -> none  [the longest x1 107 us: local(): everyone = lax.all_gather(unit_b, ('dp', 'expert'), axis=0, tiled=True)]
    all_to_all x4 -> x0, blocking collectives: 142 us -> none  [the longest x2 72.1 us: to_experts(): lax.all_to_all(packed, 'expert', split_axis=0, concat_axis=0, tiled=True)]
    all_to_all x2 -> x0, waiting for transfers between devices: 42.2 us -> none  [from_experts(): lax.all_to_all(packed, 'expert', split_axis=0, concat_axis=0, tiled=True)]
    all_to_all x2 -> x0, starting transfers between devices: 31.1 us -> none  [from_experts(): lax.all_to_all(packed, 'expert', split_axis=0, concat_axis=0, tiled=True)]
    dot_general x7 -> x4, matrix products: 27.8 us -> 6.08 us  [the longest x2 3.63 us: from_slots(): jnp.einsum('st,sd->td', slot_table, matrix_rows, preferred_element_type=j...]
    slice x1 -> x0, local copies, waits for them, and re-layouts: 6.48 us -> none  [local(): texts_all = everyone[:, 1]]
    reshape x8 -> x0, local copies, waits for them, and re-layouts: 5.35 us -> none  [the longest x2 2.19 us: to_experts(): return arrived.reshape(slot_table.shape[0], matrix_rows.shape[1])]
  transfers between devices with their start and end apart: 5 -> 0, of which waited for: 5 -> 0; matrix products, arithmetic and copies ran while one was open for 0% -> 0% of each run, Pallas kernels for 0% -> 0%
where the time goes in v1:
time: 250 us
  Pallas kernels  226 us (90%)
  matrix products  10.5 us (4%)
  other arithmetic  7.37 us (3%)
  between operations  4.58 us (2%)
    pallas_call x2, Pallas kernels, moe_call(): pl.pallas_call(functools.partial(moe_kernel, backward, ny, nz), out_shape...  190 us
    pallas_call x1, Pallas kernels, gather_call(): pl.pallas_call(functools.partial(gather_kernel, ny, nz), out_shape=jax.Sh...  35.5 us

profile of v1, /device:TPU:1, one launch (start us, length us, event | category | flops | bytes accessed | tf_op | source)
XLA Modules:
  0.0 249.6 jit_solution(4702129019948601073)
XLA Ops:
  0.6 0.0 copy-start
  0.6 0.0 copy-start.1
  0.7 0.0 copy-start.3
  0.7 0.0 copy-start.4
  0.7 0.0 copy-start.5
  0.7 0.7 convert_element_type.75
  1.4 1.1 convert_reduce_fusion
  2.5 1.2 fusion.29
  3.8 0.0 copy-done
  3.8 1.3 fusion.68
  5.1 0.0 copy-done.3
  5.2 0.0 copy-done.4
  5.2 0.0 copy-done.5
  5.2 0.0 copy-done.1
  5.2 1.3 convolution_convert_fusion.1.refs_0_
  6.5 99.9 %moe_fore.1 = (bf16[256,1280]{1,0:T(8,128)(2,1)}, f32[4,256,640]{2,1,0:T(8,128)}) custom-call(bf16[256,1280]{1,0:T(8,128)(2,1)} %convolution_convert_fusion.1.refs_0_, bf16[1280,640]{1,0:T(8,128)(2,1)} %bitcast.108, bf16[640,1280]{1,0:T(8,128)(2,1)} %bitcast.110), custom_call_target="tpu_custom_call" | custom-call | tf_op jit(solution)/shard_map/moe_fore/pallas_call | solution.py:318
  106.4 2.3 bitcast_reduce_fusion
  108.7 0.1 multiply_reduce_fusion.1
  108.8 0.1 fusion.59.u
  108.9 35.5 %gather_units.1 = bf16[64,16,1280]{2,1,0:T(8,128)(2,1)S(1)} custom-call(f32[2,1280]{1,0:T(2,128)S(1)} %fusion.59.u), custom_call_target="tpu_custom_call" | custom-call | tf_op jit(solution)/shard_map/gather_units/pallas_call | solution.py:431
  145.0 1.0 fusion.66
  146.0 0.4 exponential_reduce_fusion
  146.4 0.6 dynamic_slice.6
  147.0 0.1 fusion.58
  147.1 0.4 fusion.3
  147.5 1.3 fusion.60
  148.8 0.6 dynamic_slice.7
  151.2 0.4 fusion.8
  151.7 0.0 copy-start.2
  151.7 0.7 fusion.61
  152.4 0.3 fusion.11
  152.7 0.3 fusion.14
  153.1 0.1 multiply_reduce_fusion
  153.2 0.1 fusion.57
  153.3 0.0 copy-done.2
  153.3 0.1 fusion.34
  153.4 1.2 convolution_convert_fusion.refs_0_
  154.6 90.5 %moe_back.1 = bf16[256,1280]{1,0:T(8,128)(2,1)} custom-call(bf16[256,1280]{1,0:T(8,128)(2,1)} %convolution_convert_fusion.refs_0_, bf16[1280,640]{1,0:T(8,128)(2,1)} %bitcast.109, bf16[640,1280]{1,0:T(8,128)(2,1)} %bitcast.111, f32[4,256,640]{2,1,0:T(8,128)} %get-tuple-element.5.refs_3_), custom_call_target="tpu_custom_call" | custom-call | tf_op jit(solution)/shard_map/moe_back/pallas_call | solution.py:318
  245.1 1.4 fusion.38
  246.5 0.6 fusion.32
  247.2 0.3 fusion.67
  247.6 0.9 fusion.36
  (19 shorter events, 0.2 us)
Async XLA Ops:
  0.6 3.1 %copy-start = (bf16[1280,128]{1,0:T(8,128)(2,1)S(1)}, bf16[1280,128]{1,0:T(8,128)(2,1)}, u32[]{:S(2)}) copy-start(bf16[1280,128]{1,0:T(8,128)(2,1)} %param.11) | copy-start | bytes 983044
  0.6 4.6 %copy-start.1 = (bf16[1,128,1280]{2,1,0:T(8,128)(2,1)S(1)}, bf16[1,128,1280]{2,1,0:T(8,128)(2,1)}, u32[]{:S(2)}) copy-start(bf16[1,128,1280]{2,1,0:T(8,128)(2,1)} %param.9) | copy-start | bytes 983044
  0.7 4.5 %copy-start.3 = (s32[1,128]{1,0:T(1,128)S(1)}, s32[1,128]{1,0:T(1,128)}, u32[]{:S(2)}) copy-start(s32[1,128]{1,0:T(1,128)} %param.14) | copy-start | bytes 1540
  0.7 4.5 %copy-start.4 = (s32[1,128]{1,0:T(1,128)S(1)}, s32[1,128]{1,0:T(1,128)}, u32[]{:S(2)}) copy-start(s32[1,128]{1,0:T(1,128)} %param.15) | copy-start | bytes 1540
  0.7 4.5 %copy-start.5 = (s32[1,128]{1,0:T(1,128)S(1)}, s32[1,128]{1,0:T(1,128)}, u32[]{:S(2)}) copy-start(s32[1,128]{1,0:T(1,128)} %param.16) | copy-start | bytes 1540
  151.7 1.6 copy-start.2

commit v2 on v0

v2 whole, which is shorter than its diff:
```python
import functools
import math

import jax
import jax.numpy as jnp
import numpy as np
from jax import lax
from jax.experimental import pallas as pl
from jax.experimental.pallas import tpu as pltpu
from jax.sharding import PartitionSpec as P

MESH = pl.DeviceIdType.MESH
norm_eps = 1e-06
WIDTHS = (256, 256, 256, 256, 384)
SIDE = 128
AWAY = (0, 3, 1, 2)
CORES = 2
SLOTS = 2


def activation(values):
    return 0.5 * values * (1.0 + lax.erf(values * (0.5**0.5)))


def activation_slope(values):
    bell = jnp.exp(-0.5 * values * values) * 0.3989422804014327
    return 0.5 * (1.0 + lax.erf(values * (0.5**0.5))) + values * bell


def layer_norm(matrix_rows, ln_gain):
    centered = matrix_rows - jnp.mean(matrix_rows, -1, keepdims=True)
    variance = jnp.mean(centered * centered, -1, keepdims=True)
    return centered * lax.rsqrt(variance + norm_eps) * ln_gain.astype(jnp.float32)


def chip_sides(experts):
    chips = experts // CORES
    side = 1
    while side * side < chips:
        side *= 2
    return side, chips // side


def near_first(count):
    offsets = []
    for step in range(1, count // 2 + 1):
        offsets.append(step)
        if count - step != step:
            offsets.append(count - step)
    return offsets


def send(src, dst, send_sem, recv_sem, device):
    pltpu.make_async_remote_copy(
        src_ref=src,
        dst_ref=dst,
        send_sem=send_sem,
        recv_sem=recv_sem,
        device_id=device,
        device_id_type=MESH,
    ).start()


def drain(ref, sem):
    pltpu.make_async_copy(ref, ref, sem).wait()


def greet(peers):
    barrier = pltpu.get_barrier_semaphore()
    for peer in peers:
        pl.semaphore_signal(barrier, inc=1, device_id=peer, device_id_type=MESH)
    pl.semaphore_wait(barrier, len(peers))


def from_slots(slot_table, matrix_rows):
    return jnp.einsum("st,sd->td", slot_table, matrix_rows, preferred_element_type=jnp.float32)


def selector(sizes, source):
    count = math.prod(sizes)
    place = np.arange(count)
    digits = np.unravel_index(place, sizes)
    table = np.zeros((count, count), np.float32)
    table[place, source(*digits)] = 1.0
    return jnp.asarray(table, jnp.bfloat16)


def move_rows(table, values):
    return jnp.dot(table, values, preferred_element_type=jnp.float32).astype(jnp.bfloat16)


def spans(model_width):
    widths = WIDTHS
    if sum(widths) != model_width + SIDE:
        widths = (model_width // 2, model_width - model_width // 2 + SIDE)
    return [(sum(widths[:t]), widths[t]) for t in range(len(widths))]


def by_slab(rows, slab, blocks, step):
    def body(i, carry):
        for b in blocks:
            step(b, i, pl.ds(pl.multiple_of(i * slab, slab), slab))
        return carry

    lax.fori_loop(0, rows // slab, body, 0)


class Place:
    def __init__(self, ny, nz):
        self.ny, self.nz = ny, nz
        self.nzc = nz * CORES
        self.yb, self.zb = self.nzc * SLOTS, ny * SLOTS
        self.dpn = lax.axis_size("dp")
        self.x = lax.axis_index("dp")
        self.rank = lax.axis_index("expert")
        self.y, self.zc = lax.div(self.rank, self.nzc), lax.rem(self.rank, self.nzc)
        self.c = lax.rem(self.rank, CORES)
        self.z = lax.div(self.zc, CORES)
        self.right = (lax.rem(self.x + 1, self.dpn), self.rank)
        self.left = (lax.rem(self.x + self.dpn - 1, self.dpn), self.rank)
        self.first = self.y * (1 - self.c) + self.z * self.c
        self.second = self.z * (1 - self.c) + self.y * self.c
        self.sibling = (self.x, self.rank + 1 - 2 * self.c)
        self.y_peers = [lax.rem(self.y + k, ny) for k in near_first(ny)]
        self.z_peers = [lax.rem(self.zc + k, self.nzc) for k in near_first(self.nzc)]

    def at_y(self, peer):
        return (self.x, peer * self.nzc + self.zc)

    def at_z(self, peer):
        return (self.x, self.y * self.nzc + peer)

    def at_grid(self, first, second):
        c = self.c
        y_at = first * (1 - c) + second * c
        z_at = second * (1 - c) + first * c
        return (self.x, y_at * self.nzc + z_at * CORES + c)

    def at_near(self, b, core):
        return (lax.rem(self.x + AWAY[b], self.dpn), self.y * self.nzc + self.z * CORES + core)

    def y_block(self, index):
        return pl.ds(pl.multiple_of(index * self.yb, self.yb), self.yb)

    def z_block(self, index):
        return pl.ds(pl.multiple_of(index * self.zb, self.zb), self.zb)


def fore_kernel(ny, nz, spread, scale, *refs):
    src, u, w_in_far, w_out_far, perm, perm_small, perm_x, out, slope, hid, side = refs[:11]
    n = len(spread)
    bufs = [refs[11 + 6 * t : 17 + 6 * t] for t in range(n)]
    at = 11 + 6 * n
    w_in, w_out, acc, hc, hp, po, sib_out, sib_in, st, got, sums, st_b, got_b = refs[at : at + 13]
    near, block, st_c, got_c, half_block, held = refs[at + 13 : at + 19]
    s_y, r_y, s_z, r_z, s_x, r_x, s_o, r_o, s_d, r_d, s_f, r_f, s_g, r_g = refs[at + 19 : at + 33]
    s_b, r_b, s_c, r_c, load = refs[at + 33 :]
    p = Place(ny, nz)
    rows = acc.shape[1]
    half = rows // 2
    top, low = pl.ds(0, half), pl.ds(half, half)
    yb, zb = p.yb, p.zb
    half_width = po.shape[2]
    model_width = 2 * half_width

    pltpu.make_async_copy(w_in_far, w_in, load.at[0]).start()
    pltpu.make_async_copy(w_out_far, w_out, load.at[1]).start()
    others = [p.at_near(b, core) for b in range(1, 4) for core in range(CORES)]
    greet([p.at_y(peer) for peer in p.y_peers] + [p.at_z(peer) for peer in p.z_peers] + others)

    for t, (start, width) in enumerate(spread):
        for peer in p.y_peers:
            send(
                src.at[p.y_block(peer), pl.ds(start, width)],
                bufs[t][0].at[p.y_block(p.y)],
                s_y.at[t],
                r_y.at[t],
                p.at_y(peer),
            )

    own_near = p.x * CORES + p.c
    near_count = 4 * CORES
    for peer in others + [p.sibling]:
        send(u, near.at[own_near], s_g.at[0], r_g.at[0], peer)
    near[own_near] = u[...]

    def stage_z(t):
        ybuf, zsend, zbuf = bufs[t][:3]
        start, width = spread[t]
        ybuf[p.y_block(p.y), :] = src[p.y_block(p.y), start : start + width]
        drain(ybuf.at[pl.ds(0, rows - yb)], r_y.at[t])
        zsend[...] = move_rows(perm[0], ybuf[...])
        for peer in p.z_peers:
            send(zsend.at[p.z_block(peer)], zbuf.at[p.z_block(p.zc)], s_z.at[t], r_z.at[t], p.at_z(peer))
        zbuf[p.z_block(p.zc), :] = zsend[p.z_block(p.zc), :]

    def stage_x(t):
        zbuf, xl, xr = bufs[t][2:5]
        drain(zbuf.at[pl.ds(0, rows - zb)], r_z.at[t])
        send(zbuf, xl, s_x.at[t, 0], r_x.at[t, 0], p.right)
        send(zbuf, xr, s_x.at[t, 1], r_x.at[t, 1], p.left)

    def stage_forward(t):
        xl, xr, xo = bufs[t][3:6]
        drain(xl, r_x.at[t, 0])
        send(xl.at[top], xo.at[top], s_o.at[t, 0], r_o.at[t, 0], p.right)
        drain(xr, r_x.at[t, 1])
        send(xr.at[low], xo.at[low], s_o.at[t, 1], r_o.at[t, 1], p.left)

    def stage_in(t, b):
        start, width = spread[t]
        depth = min(start + width, model_width) - start
        values = bufs[t][2 + b]
        part = jnp.dot(values[:, :depth], w_in[start : start + depth, :], preferred_element_type=jnp.float32)
        acc[b] = part if t == 0 else acc[b] + part
        if t == n - 1:
            side[b] = values[:, depth:]

    def await_far(t):
        xo = bufs[t][5]
        drain(xo.at[top], r_o.at[t, 0])
        drain(xo.at[low], r_o.at[t, 1])

    for t in range(n + 2):
        if t < n:
            stage_z(t)
        if 0 <= t - 1 < n:
            stage_x(t - 1)
        if 0 <= t - 2 < n:
            stage_forward(t - 2)
        if t == 2:
            pltpu.make_async_copy(w_in_far, w_in, load.at[0]).wait()
        if 0 <= t - 3 < n - 1:
            await_far(t - 3)
            for b in range(4):
                stage_in(t - 3, b)

    def hidden_step(b, i, rows_at):
        values = activation(acc[b, rows_at, :])
        hid[b, rows_at, :] = values.astype(jnp.bfloat16)
        gates = side[b, rows_at, :].astype(jnp.float32)
        image = values * (gates[:, 0:1] + gates[:, 1:2])
        text = values * (gates[:, 2:3] + gates[:, 3:4])
        both = jnp.concatenate([image[:ny] + image[ny:], text[:ny] + text[ny:]], 0)
        hc[b, rows_at, :] = both.astype(jnp.bfloat16)

    def half_cols(core):
        return pl.ds(pl.multiple_of(core * half_width, half_width), half_width)

    other = 1 - p.c
    line = [lax.rem(p.first + k, ny) for k in near_first(ny)]

    def stage_line(b):
        drain(sib_in.at[b], r_d.at[b])
        st[b] = (po[b] + sib_in[b].astype(jnp.float32)).astype(jnp.bfloat16)
        for peer in line:
            send(
                st.at[b, p.y_block(peer)], got.at[b, p.first], s_f.at[b], r_f.at[b], p.at_grid(peer, p.second)
            )
        got[b, p.first] = st[b, p.y_block(p.first), :]

    pltpu.make_async_copy(w_out_far, w_out, load.at[1]).wait()
    for b in range(4):
        if b == 3:
            await_far(n - 1)
        stage_in(n - 1, b)
        by_slab(rows, zb, [b], hidden_step)
        hp[0] = move_rows(perm[1 + other], hc[b])
        sib_out[b] = jnp.dot(hp[0], w_out[:, half_cols(other)], preferred_element_type=jnp.float32).astype(
            jnp.bfloat16
        )
        send(sib_out.at[b], sib_in.at[b], s_d.at[b], r_d.at[b], p.sibling)
        hp[1] = move_rows(perm[1 + p.c], hc[b])
        po[b] = jnp.dot(hp[1], w_out[:, half_cols(p.c)], preferred_element_type=jnp.float32)
        if b > 0:
            stage_line(b - 1)
    stage_line(3)

    def slope_step(b, i, rows_at):
        slope[b, rows_at, :] = activation_slope(acc[b, rows_at, :])

    by_slab(rows, zb, range(2), slope_step)

    for b in range(4):
        drain(got.at[b, pl.ds(0, ny - 1)], r_f.at[b])
        total = got[b, 0].astype(jnp.float32)
        for k in range(1, ny):
            total = total + got[b, k].astype(jnp.float32)
        sums[b * yb : (b + 1) * yb, :] = total.astype(jnp.bfloat16)
    st_b[...] = move_rows(perm_small[...], sums[...])
    cut = 4 * CORES * 2

    def cut_block(index):
        return pl.ds(pl.multiple_of(index * cut, cut), cut)

    for k in near_first(ny):
        peer = lax.rem(p.second + k, ny)
        send(st_b.at[cut_block(peer)], got_b.at[p.second], s_g.at[1], r_g.at[1], p.at_grid(p.first, peer))
    got_b[p.second] = st_b[cut_block(p.second), :]
    drain(got_b.at[pl.ds(0, ny - 1)], r_g.at[1])
    total = got_b[0].astype(jnp.float32)
    for k in range(1, ny):
        total = total + got_b[k].astype(jnp.float32)
    part_rows = CORES * 2
    for b in range(4):
        st_c[lax.rem(p.x + AWAY[b], 4)] = total[b * part_rows : (b + 1) * part_rows]
    for b in range(1, 4):
        send(st_c, got_c.at[p.x], s_g.at[2], r_g.at[2], p.at_near(b, p.c))
    got_c[p.x] = st_c[...]
    drain(near.at[pl.ds(0, near_count - 1)], r_g.at[0])
    for k in range(near_count):
        for m in range(2):
            block[m * near_count + k : m * near_count + k + 1, :] = near[k, m : m + 1, :]
    drain(got_c.at[pl.ds(0, 3)], r_g.at[2])
    total = got_c[0] + got_c[1] + got_c[2] + got_c[3]
    for k in range(near_count):
        for m in range(2):
            row = m * near_count + k
            half_sum = jnp.where(p.c == 0, block[row : row + 1, :half_width], block[row : row + 1, half_width:])
            block[row : row + 1, :half_width] = half_sum + total[k // CORES, k % CORES * 2 + m][None]
    half_block[...] = (block[:, :half_width] * scale).astype(jnp.bfloat16)

    c, side_len, second = p.c, ny, p.second
    held[c, second, p.first] = half_block[...]
    for peer in line:
        send(half_block, held.at[c, second, p.first], s_g.at[3], r_g.at[3], p.at_grid(peer, second))
    drain(held.at[c, second, pl.ds(0, side_len - 1)], r_g.at[3])

    def share(slab, k):
        send(slab, slab, s_c.at[k], r_c.at[k], p.sibling)

    share(held.at[c, second], 0)
    right = p.at_grid(p.first, lax.rem(second + 1, side_len))
    left = p.at_grid(p.first, lax.rem(second + side_len - 1, side_len))
    full = side_len // 2 - 1
    for i in range(full):
        r_slab = held.at[c, lax.rem(second + side_len - i, side_len)]
        l_slab = held.at[c, lax.rem(second + i, side_len)]
        send(r_slab, r_slab, s_b.at[i, 0], r_b.at[i, 0], right)
        send(l_slab, l_slab, s_b.at[i, 1], r_b.at[i, 1], left)
        if i == 0:
            by_slab(rows, zb, range(2, 4), slope_step)
        for way, here in enumerate((second + side_len - i - 1, second + i + 1)):
            slab = held.at[c, lax.rem(here, side_len)]
            drain(slab, r_b.at[i, way])
            share(slab, 1 + 2 * i + way)
    parts = (pl.ds(0, side_len // 2), pl.ds(side_len // 2, side_len // 2))
    r_slab = held.at[c, lax.rem(second + side_len - full, side_len), parts[0]]
    l_slab = held.at[c, lax.rem(second + full, side_len), parts[1]]
    send(r_slab, r_slab, s_b.at[full, 0], r_b.at[full, 0], right)
    send(l_slab, l_slab, s_b.at[full, 1], r_b.at[full, 1], left)
    if full == 0:
        by_slab(rows, zb, range(2, 4), slope_step)
    for way in range(2):
        slab = held.at[c, lax.rem(second + side_len // 2, side_len), parts[way]]
        drain(slab, r_b.at[full, way])
        share(slab, 1 + 2 * full + way)
    for k in range(1 + 2 * full):
        drain(held.at[0, 0], r_c.at[k])
    for way in range(2):
        drain(held.at[0, 0, parts[way]], r_c.at[1 + 2 * full + way])
    span = CORES * side_len
    for h in range(CORES):
        for z_at in range(side_len):
            slab = held[h, z_at] if h == 0 else held[h, :, z_at]
            moved = move_rows(perm_x[p.x], slab.reshape(side_len * 2 * near_count, half_width))
            for k in range(2 * 4):
                out[k // 4, k % 4, z_at * span : (z_at + 1) * span, h * half_width : (h + 1) * half_width] = moved[
                    k * span : (k + 1) * span
                ]

    for t in range(n):
        ybuf, zsend, zbuf, xl, xr, xo = bufs[t]
        drain(ybuf.at[pl.ds(0, rows - yb)], s_y.at[t])
        drain(zsend.at[pl.ds(0, rows - zb)], s_z.at[t])
        for way in range(2):
            drain(zbuf, s_x.at[t, way])
            drain(xo.at[top], s_o.at[t, way])
    for b in range(4):
        drain(sib_out.at[b], s_d.at[b])
        drain(got.at[b, pl.ds(0, ny - 1)], s_f.at[b])
    drain(near.at[pl.ds(0, near_count - 1)], s_g.at[0])
    drain(got_b.at[pl.ds(0, ny - 1)], s_g.at[1])
    drain(got_c.at[pl.ds(0, 3)], s_g.at[2])
    drain(held.at[0, 0, pl.ds(0, ny - 1)], s_g.at[3])
    for way in range(2):
        for i in range(full):
            drain(held.at[0, 0], s_b.at[i, way])
        drain(held.at[0, 0, parts[way]], s_b.at[full, way])
        drain(held.at[0, 0, parts[way]], s_c.at[1 + 2 * full + way])
    for k in range(1 + 2 * full):
        drain(held.at[0, 0], s_c.at[k])


def fore_call(experts, seq_len, packed, u, w_in, w_out):
    ny, nz = chip_sides(experts)
    rows = packed.shape[0]
    model_width, hidden = w_in.shape
    half_width = model_width // 2
    spread = spans(model_width)
    n = len(spread)
    yb, zb, cut = nz * CORES * SLOTS, ny * SLOTS, 4 * CORES * 2
    bf16, f32 = jnp.bfloat16, jnp.float32
    vmem = pl.BlockSpec(memory_space=pltpu.VMEM)
    far = pl.BlockSpec(memory_space=pl.ANY)
    dma = pltpu.SemaphoreType.DMA
    perm = jnp.stack(
        [
            selector((nz * CORES, SLOTS, ny), lambda zc, s, ys: ys * yb + zc * SLOTS + s),
            selector((ny, nz, CORES, 2), lambda ys, zs, cs, m: (zs * CORES + cs) * zb + m * ny + ys),
            selector((nz, ny, CORES, 2), lambda zs, ys, cs, m: (zs * CORES + cs) * zb + m * ny + ys),
        ]
    )
    perm_small = selector((ny, 4, CORES, 2), lambda second, b, cs, m: b * yb + second * 4 + cs * 2 + m)
    perm_x = jnp.stack(
        [
            selector(
                (2, 4, CORES, ny),
                lambda m, b, cs, ys: ys * cut + m * 4 * CORES + (x + np.array(AWAY)[b]) % 4 * CORES + cs,
            )
            for x in range(4)
        ]
    )
    scratch = [pltpu.VMEM((rows, width), bf16) for _, width in spread for _ in range(6)]
    scratch += [
        pltpu.VMEM(w_in.shape, bf16),
        pltpu.VMEM(w_out.shape, bf16),
        pltpu.VMEM((4, rows, hidden), f32),
        pltpu.VMEM((4, rows, hidden), bf16),
        pltpu.VMEM((2, rows, hidden), bf16),
        pltpu.VMEM((4, rows, half_width), f32),
        pltpu.VMEM((4, rows, half_width), bf16),
        pltpu.VMEM((4, rows, half_width), bf16),
        pltpu.VMEM((4, rows, half_width), bf16),
        pltpu.VMEM((4, ny, yb, half_width), bf16),
        pltpu.VMEM((4 * yb, half_width), bf16),
        pltpu.VMEM((4 * yb, half_width), bf16),
        pltpu.VMEM((ny, cut, half_width), bf16),
        pltpu.VMEM((4 * CORES, 2, model_width), f32),
        pltpu.VMEM((cut, model_width), f32),
        pltpu.VMEM((4, CORES * 2, half_width), f32),
        pltpu.VMEM((4, 4, CORES * 2, half_width), f32),
        pltpu.VMEM((cut, half_width), bf16),
        pltpu.VMEM((CORES, nz, ny, cut, half_width), bf16),
    ]
    steps = ny // 2
    scratch += [dma((n,)) for _ in range(4)] + [dma((n, 2)) for _ in range(4)]
    scratch += [dma((4,)) for _ in range(6)]
    scratch += [dma((steps, 2)) for _ in range(2)] + [dma((2 * steps + 1,)) for _ in range(2)] + [dma((2,))]
    return pl.pallas_call(
        functools.partial(fore_kernel, ny, nz, spread, 1.0 / seq_len),
        out_shape=[
            jax.ShapeDtypeStruct((2, 4, experts, model_width), bf16),
            jax.ShapeDtypeStruct((4, rows, hidden), f32),
            jax.ShapeDtypeStruct((4, rows, hidden), bf16),
            jax.ShapeDtypeStruct((4, rows, SIDE), bf16),
        ],
        in_specs=[vmem, vmem, far, far, vmem, vmem, vmem],
        out_specs=[vmem] * 4,
        scratch_shapes=scratch,
        name="moe_fore",
        compiler_params=pltpu.CompilerParams(
            collective_id=0, has_side_effects=True, vmem_limit_bytes=56 * 1024 * 1024
        ),
    )(packed, u, w_in, w_out, perm, perm_small, perm_x)


def back_kernel(ny, nz, spread, *refs):
    d_all, w_in_far, w_out, slope_far, hid_far, side, perm, out = refs[:8]
    n = len(spread)
    bufs = [refs[8 + 12 * t : 20 + 12 * t] for t in range(n)]
    at = 8 + 12 * n
    pulled, d_pre, d_gate, w_in, slope, hid = refs[at : at + 6]
    s_p, r_p, s_q, r_q, s_z, r_z, s_y, r_y, load = refs[at + 6 :]
    loads = [
        pltpu.make_async_copy(w_in_far, w_in, load.at[0]),
        pltpu.make_async_copy(slope_far, slope, load.at[1]),
        pltpu.make_async_copy(hid_far, hid, load.at[2]),
    ]
    for copy in (loads[1], loads[2], loads[0]):
        copy.start()
    p = Place(ny, nz)
    rows = slope_far.shape[1]
    half = rows // 2
    top, low = pl.ds(0, half), pl.ds(half, half)
    yb, zb = p.yb, p.zb
    model_width = w_in_far.shape[0]
    pairs = d_all.shape[1]

    greet(
        [p.at_y(peer) for peer in p.y_peers] + [p.at_z(peer) for peer in p.z_peers] + [p.right, p.left]
    )

    def pull(b):
        part = pl.ds(b * (pairs // 4), pairs // 4)
        for m in range(2):
            pulled[m, part, :] = lax.dot_general(
                d_all[m, part, :], w_out[...], (((1,), (1,)), ((), ())), preferred_element_type=jnp.float32
            )

    def pre_step(b, i, rows_at):
        pair_at = pl.ds(pl.multiple_of(b * (pairs // 4) + i * ny, ny), ny)
        gates = side[b, rows_at, :].astype(jnp.float32)
        image = pulled[0, pair_at, :]
        text = pulled[1, pair_at, :]
        d_act = jnp.concatenate([image, image], 0) * (gates[:, 0:1] + gates[:, 1:2])
        d_act = d_act + jnp.concatenate([text, text], 0) * (gates[:, 2:3] + gates[:, 3:4])
        d_pre[b, rows_at, :] = (d_act * slope[b, rows_at, :]).astype(jnp.bfloat16)
        value = jnp.sum(d_act * hid[b, rows_at, :].astype(jnp.float32), 1, keepdims=True)
        high = value.astype(jnp.bfloat16).astype(jnp.float32)
        lane = lax.broadcasted_iota(jnp.int32, (zb, SIDE), 1)
        d_gate[b, rows_at, :] = jnp.where(
            lane == 2 * p.x, high, jnp.where(lane == 2 * p.x + 1, value - high, 0.0)
        )

    def product_out(b, t):
        start, width = spread[t]
        depth = min(start + width, model_width) - start
        part = lax.dot_general(
            d_pre[b], w_in[start : start + depth, :], (((1,), (1,)), ((), ())), preferred_element_type=jnp.float32
        )
        if t == n - 1:
            part = jnp.concatenate([part, d_gate[b]], 1)
        return part

    def stage_far(t):
        so, sr, sl, ol, orr = bufs[t][:5]
        so[...] = product_out(3, t).astype(jnp.bfloat16)
        send(so.at[top], ol, s_p.at[t, 0], r_p.at[t, 0], p.right)
        send(so.at[low], orr, s_p.at[t, 1], r_p.at[t, 1], p.left)

    def stage_near(t):
        so, sr, sl, ol, orr, fl, fr, zs, zr, ys, yr, own = bufs[t]
        part = product_out(2, t)
        sr[half:, :] = part[half:].astype(jnp.bfloat16)
        drain(ol, r_p.at[t, 0])
        sr[:half, :] = (part[:half] + ol[...].astype(jnp.float32)).astype(jnp.bfloat16)
        send(sr, fl, s_q.at[t, 0], r_q.at[t, 0], p.right)
        part = product_out(1, t)
        sl[:half, :] = part[:half].astype(jnp.bfloat16)
        drain(orr, r_p.at[t, 1])
        sl[half:, :] = (part[half:] + orr[...].astype(jnp.float32)).astype(jnp.bfloat16)
        send(sl, fr, s_q.at[t, 1], r_q.at[t, 1], p.left)
        own[...] = product_out(0, t)

    def stage_back_z(t):
        so, sr, sl, ol, orr, fl, fr, zs, zr, ys, yr, own = bufs[t]
        drain(fl, r_q.at[t, 0])
        drain(fr, r_q.at[t, 1])
        zs[...] = (own[...] + fl[...].astype(jnp.float32) + fr[...].astype(jnp.float32)).astype(jnp.bfloat16)
        for peer in p.z_peers:
            send(zs.at[p.z_block(peer)], zr.at[p.z_block(p.zc)], s_z.at[t], r_z.at[t], p.at_z(peer))
        zr[p.z_block(p.zc), :] = zs[p.z_block(p.zc), :]

    def stage_back_y(t):
        zr, ys, yr = bufs[t][8:11]
        drain(zr.at[pl.ds(0, rows - zb)], r_z.at[t])
        ys[...] = move_rows(perm[...], zr[...])
        for peer in p.y_peers:
            send(ys.at[p.y_block(peer)], yr.at[p.y_block(p.y)], s_y.at[t], r_y.at[t], p.at_y(peer))
        yr[p.y_block(p.y), :] = ys[p.y_block(p.y), :]

    def stage_store(t):
        yr = bufs[t][10]
        start, width = spread[t]
        drain(yr.at[pl.ds(0, rows - yb)], r_y.at[t])
        out[:, start : start + width] = yr[...]

    pull(3)
    loads[1].wait()
    loads[2].wait()
    by_slab(rows, zb, [3], pre_step)
    loads[0].wait()
    for t in range(n):
        stage_far(t)
    for b in range(3):
        pull(b)
    by_slab(rows, zb, range(3), pre_step)
    for t in range(n + 3):
        if t < n:
            stage_near(t)
        if 0 <= t - 1 < n:
            stage_back_z(t - 1)
        if 0 <= t - 2 < n:
            stage_back_y(t - 2)
        if 0 <= t - 3 < n:
            stage_store(t - 3)

    for t in range(n):
        so, sr, sl, ol, orr, fl, fr, zs, zr, ys, yr, own = bufs[t]
        drain(zs.at[pl.ds(0, rows - zb)], s_z.at[t])
        drain(ys.at[pl.ds(0, rows - yb)], s_y.at[t])
        for way in range(2):
            drain(so.at[top], s_p.at[t, way])
            drain(sr, s_q.at[t, way])


def back_call(experts, d_all, w_in, w_out, slope, hid, side):
    ny, nz = chip_sides(experts)
    rows = slope.shape[1]
    model_width, hidden = w_in.shape
    spread = spans(model_width)
    n = len(spread)
    half = rows // 2
    bf16, f32 = jnp.bfloat16, jnp.float32
    vmem = pl.BlockSpec(memory_space=pltpu.VMEM)
    dma = pltpu.SemaphoreType.DMA
    scratch = []
    for _, width in spread:
        scratch += [pltpu.VMEM((rows, width), bf16) for _ in range(3)]
        scratch += [pltpu.VMEM((half, width), bf16) for _ in range(2)]
        scratch += [pltpu.VMEM((rows, width), bf16) for _ in range(6)]
        scratch += [pltpu.VMEM((rows, width), f32)]
    scratch += [
        pltpu.VMEM((2, d_all.shape[1], hidden), f32),
        pltpu.VMEM((4, rows, hidden), bf16),
        pltpu.VMEM((4, rows, SIDE), f32),
        pltpu.VMEM(w_in.shape, bf16),
        pltpu.VMEM(slope.shape, f32),
        pltpu.VMEM(hid.shape, bf16),
    ]
    scratch += [dma((n, 2)) for _ in range(4)] + [dma((n,)) for _ in range(4)] + [dma((3,))]
    yb, zb = nz * CORES * SLOTS, ny * SLOTS
    perm = selector((ny, nz * CORES, SLOTS), lambda ys, zc, s: zc * zb + s * ny + ys)
    far = pl.BlockSpec(memory_space=pl.ANY)
    return pl.pallas_call(
        functools.partial(back_kernel, ny, nz, spread),
        out_shape=jax.ShapeDtypeStruct((rows, model_width + SIDE), bf16),
        in_specs=[vmem, far, vmem, far, far, vmem, vmem],
        out_specs=vmem,
        scratch_shapes=scratch,
        name="moe_back",
        compiler_params=pltpu.CompilerParams(
            collective_id=1, has_side_effects=True, vmem_limit_bytes=56 * 1024 * 1024
        ),
    )(d_all, w_in, w_out, slope, hid, side, perm)


def local(tokens, ln_gain, w_router, w_in, w_out, expert_ids, keep, slots, logit_scale):
    pairs_dev, row_width, model_width = tokens.shape
    seq_len = row_width // 2
    token_count = pairs_dev * row_width
    experts = w_router.shape[1]
    capacity = SLOTS
    score_scale = logit_scale[0]
    rows_in = tokens.reshape(token_count, model_width).astype(jnp.float32)
    normed, norm_pull = jax.vjp(lambda values: layer_norm(values, ln_gain), rows_in)
    normed_b = normed.astype(jnp.bfloat16)
    routed = expert_ids.reshape(token_count)
    keep_flat = keep.reshape(token_count)
    target = routed * capacity + slots.reshape(token_count)
    slot_iota = lax.broadcasted_iota(jnp.int32, (experts * capacity, token_count), 0)
    slot_table = ((slot_iota == target[None, :]) & (keep_flat[None, :] == 1)).astype(jnp.bfloat16)
    choose = (lax.broadcasted_iota(jnp.int32, (token_count, experts), 1) == routed[:, None]).astype(
        jnp.float32
    )
    logits = jnp.dot(normed_b, w_router, preferred_element_type=jnp.float32)
    expo = jnp.exp(logits)
    probs = expo / jnp.sum(expo, 1, keepdims=True)
    gate_val = jnp.sum(probs * choose, 1, keepdims=True)
    high = gate_val.astype(jnp.bfloat16).astype(jnp.float32)
    lane = lax.broadcasted_iota(jnp.int32, (token_count, SIDE), 1)
    modality = lax.broadcasted_iota(jnp.int32, (token_count, SIDE), 0) // seq_len
    gate_side = jnp.where(
        lane == 2 * modality, high, jnp.where(lane == 2 * modality + 1, gate_val - high, 0.0)
    ).astype(jnp.bfloat16)
    packed = jnp.dot(
        slot_table, jnp.concatenate([normed_b, gate_side], 1), preferred_element_type=jnp.float32
    ).astype(jnp.bfloat16)
    token_sums = jnp.sum(rows_in.reshape(2, seq_len, model_width), 1)
    everyone, slope, hid, side = fore_call(experts, seq_len, packed, token_sums, w_in[0], w_out[0])
    everyone = everyone.reshape(2, -1, model_width)
    pair_count = everyone.shape[1]
    all_f = everyone.astype(jnp.float32)
    inverse = lax.rsqrt(jnp.sum(all_f * all_f, -1) + norm_eps)
    ny, nz = chip_sides(experts)
    rank = lax.axis_index("expert")
    own_index = (rank % (nz * CORES)) * ny + rank // (nz * CORES)
    scores = (
        jnp.einsum("id,jd->ij", everyone[0], everyone[1], preferred_element_type=jnp.float32)
        * (score_scale * inverse[0])[:, None]
        * inverse[1][None, :]
    )
    row_tot = jax.nn.logsumexp(scores, 1)
    col_tot = jax.nn.logsumexp(scores, 0)
    row_iota = lax.broadcasted_iota(jnp.int32, (pair_count, pair_count), 0)
    eye = (row_iota == lax.broadcasted_iota(jnp.int32, (pair_count, pair_count), 1)).astype(jnp.float32)
    diag_score = jnp.sum(scores * eye, 1)
    losses = (row_tot + col_tot - 2.0 * diag_score) * 0.5
    pair_loss = lax.dynamic_slice_in_dim(losses, own_index, pairs_dev)
    weights = (jnp.exp(scores - row_tot[:, None]) + jnp.exp(scores - col_tot[None, :])) * 0.5 - eye
    d_images = jnp.dot(
        (weights * inverse[1][None, :]).astype(jnp.bfloat16), everyone[1], preferred_element_type=jnp.float32
    )
    d_texts = lax.dot_general(
        (weights * inverse[0][:, None]).astype(jnp.bfloat16),
        everyone[0],
        (((0,), (0,)), ((), ())),
        preferred_element_type=jnp.float32,
    )
    d_units = jnp.stack([d_images, d_texts])
    units = all_f * inverse[:, :, None]
    along = jnp.sum(d_units * units, -1, keepdims=True)
    d_pooled = (d_units - units * along) * (inverse * (score_scale / seq_len))[:, :, None]
    d_own = lax.dynamic_slice_in_dim(d_pooled, own_index, pairs_dev, 1)
    d_mixed = jnp.broadcast_to(d_own, (2, seq_len, model_width)).reshape(token_count, model_width)
    d_back = back_call(experts, d_pooled.astype(jnp.bfloat16), w_in[0], w_out[0], slope, hid, side)
    d_slots = jnp.einsum("st,sd->td", slot_table, d_back, preferred_element_type=jnp.float32)
    d_gate = jnp.sum(d_slots[:, model_width : model_width + 8], 1)
    d_logit = d_gate[:, None] * (choose - probs)
    router_part = jnp.dot(d_logit, w_router.astype(jnp.float32).T, precision=lax.Precision.HIGHEST)
    d_normed = d_slots[:, :model_width] + router_part
    d_tokens = d_mixed + norm_pull(d_normed)[0]
    tokens_grad = (d_tokens * (128.0 * seq_len / score_scale)).astype(jnp.bfloat16)
    return (pair_loss, tokens_grad.reshape(pairs_dev, row_width, model_width))


def solution(mesh):
    in_specs = (
        P(("dp", "expert"), None, None),
        P(),
        P(),
        P("expert", None, "dp"),
        P("expert", "dp", None),
        P(("dp", "expert"), None),
        P(("dp", "expert"), None),
        P(("dp", "expert"), None),
        P(),
    )
    out_specs = (P(("dp", "expert")), P(("dp", "expert"), None, None))
    return jax.shard_map(local, mesh=mesh, in_specs=in_specs, out_specs=out_specs, check_vma=False)
```

time: 469 us -> 213 us (0.45)
  waiting for transfers between devices: 218 us -> 0 us
  Pallas kernels: 0 us -> 188 us
  blocking collectives: 142 us -> 0 us
  starting transfers between devices: 31.4 us -> 0 us
  matrix products: 32.3 us -> 6.78 us
  between operations: 17.8 us -> 1.6 us
  local copies, waits for them, and re-layouts: 13.1 us -> 0.93 us
    pallas_call x0 -> x2, Pallas kernels: none -> 188 us  [the longest x1 125 us: fore_call(): pl.pallas_call(functools.partial(fore_kernel, ny, nz, spread, 1.0 / seq_l...]
    all_gather x3 -> x0, waiting for transfers between devices: 175 us -> none  [the longest x1 107 us: local(): everyone = lax.all_gather(unit_b, ('dp', 'expert'), axis=0, tiled=True)]
    all_to_all x4 -> x0, blocking collectives: 142 us -> none  [the longest x2 72.1 us: to_experts(): lax.all_to_all(packed, 'expert', split_axis=0, concat_axis=0, tiled=True)]
    all_to_all x2 -> x0, waiting for transfers between devices: 42.2 us -> none  [from_experts(): lax.all_to_all(packed, 'expert', split_axis=0, concat_axis=0, tiled=True)]
    all_to_all x2 -> x0, starting transfers between devices: 31.1 us -> none  [from_experts(): lax.all_to_all(packed, 'expert', split_axis=0, concat_axis=0, tiled=True)]
    dot_general x12 -> x5, matrix products: 30.3 us -> 5.82 us  [the longest x1 1.43 us: local(): jnp.einsum('st,sd->td', slot_table, d_back, preferred_element_type=jnp.fl...]
    slice x1, local copies, waits for them, and re-layouts: 6.48 us -> 0.17 us  [local(): everyone[1]]
    reshape x8 -> x0, local copies, waits for them, and re-layouts: 5.35 us -> none  [the longest x2 2.19 us: to_experts(): return arrived.reshape(slot_table.shape[0], matrix_rows.shape[1])]
  transfers between devices with their start and end apart: 5 -> 0, of which waited for: 5 -> 0; matrix products, arithmetic and copies ran while one was open for 0% -> 0% of each run, Pallas kernels for 0% -> 0%
where the time goes in v2:
time: 213 us; the launch traced here: 212 us
  Pallas kernels  188 us (88%)
  other arithmetic  15.6 us (7%)
  matrix products  6.78 us (3%)
    pallas_call x1, Pallas kernels, fore_call(): pl.pallas_call(functools.partial(fore_kernel, ny, nz, spread, 1.0 / seq_l...  125 us
    pallas_call x1, Pallas kernels, back_call(): pl.pallas_call(functools.partial(back_kernel, ny, nz, spread), out_shape=...  62.1 us

profile of v2, /device:TPU:1, one launch (start us, length us, event | category | flops | bytes accessed | tf_op | source)
XLA Modules:
  0.0 212.4 jit_solution(15198526100029941399)
XLA Ops:
  0.6 0.0 copy-start
  1.4 0.7 compare_bitcast_fusion
  2.1 0.7 add_bitcast_fusion
  2.7 1.1 convert_reduce_fusion
  3.8 1.2 multiply_reduce_fusion.2
  5.1 0.7 convert_element_type.82
  5.8 1.6 reduce_sum.129.refs_1_
  7.4 1.2 multiply_convert_fusion.2
  8.6 0.0 copy-done
  8.6 0.3 fusion.45
  9.0 0.7 select_reduce_fusion.1
  9.7 0.1 copy.20
  9.8 1.2 convolution_convert_fusion.refs_0_
  11.0 125.4 %moe_fore.1 = (bf16[2,4,128,1280]{3,2,1,0:T(8,128)(2,1)}, f32[4,256,640]{2,1,0:T(8,128)}, bf16[4,256,640]{2,1,0:T(8,128)(2,1)}, bf16[4,256,128]{2,1,0:T(8,128)(2,1)}) custom-call(bf16[256,1408]{1,0:T(8,128)(2,1)} %convolution_convert_fusion.refs_0_, f32[2,1280]{1,0:T(2,128)} %reduce_sum.129.refs_1_, bf16[1280,640]{1,0:T(8,128)(2,1)} %bitcast.77, ...), custom_call_target="tpu_custom_call" | custom-call | tf_op jit(solution)/shard_map/moe_fore/pallas_call | solution.py:450
  136.5 0.0 copy-start.1
  136.5 2.5 %multiply_reduce_fusion = f32[2,4,128]{2,1,0:T(4,128)S(1)} fusion(bf16[2,4,128,1280]{3,2,1,0:T(8,128)(2,1)} %get-tuple-element.6), kind=kLoop, calls=%fused_computation.6 | loop fusion | flops 3931136 | bytes 2625536 | tf_op jit(solution)/shard_map/reduce_sum | solution.py:675
  139.0 0.0 copy-done.1
  139.0 0.2 fusion.44
  139.2 1.0 fusion.40
  140.2 0.4 exponential_reduce_fusion
  140.6 0.6 dynamic_slice.6
  141.2 1.1 fusion.7
  142.3 1.1 fusion.8
  143.4 0.8 fusion.1
  144.3 2.6 %fusion.42 = (bf16[2,512,1280]{2,1,0:T(8,128)(2,1)}, f32[2,512,1280]{2,1,0:T(8,128)S(1)}) fusion(f32[2,512]{1,0:T(2,128)S(1)} %broadcast_multiply_fusion, f32[2,512]{1,0:T(2,128)S(1)} %bitcast.89, f32[2,512]{1,0:T(2,128)S(1)} %bitcast.88, bf16[2,4,128,1280]{3,2,1,0:T(8,128)(2,1)S(1)} %copy-done.1, f32[1,512,1280]{2,1,0:T(8,128)S(1)} %bitcast.76, ...), kind=kLoop, calls=%fused_computation.96 | loop fusion | flops 9175040 | bytes 15740928 | tf_op jit(solution)/shard_map/convert_element_type | solution.py:707
  146.9 0.0 copy-start.2
  146.9 0.0 copy-start.3
  146.9 62.1 %moe_back.1 = bf16[256,1408]{1,0:T(8,128)(2,1)} custom-call(bf16[2,512,1280]{2,1,0:T(8,128)(2,1)} %get-tuple-element.17.refs_0_, bf16[1280,640]{1,0:T(8,128)(2,1)} %bitcast.78, bf16[640,1280]{1,0:T(8,128)(2,1)} %bitcast.80, f32[4,256,640]{2,1,0:T(8,128)} %get-tuple-element.7.refs_3_, bf16[4,256,640]{2,1,0:T(8,128)(2,1)} %get-tuple-element.8.refs_4_, ...), custom_call_target="tpu_custom_call" | custom-call | tf_op jit(solution)/shard_map/moe_back/pallas_call | solution.py:626
  209.0 1.4 fusion.21
  210.4 0.1 slice_reduce_fusion
  210.5 0.0 copy-done.2
  210.5 0.0 copy-done.3
  210.6 0.6 multiply_reduce_fusion.1
  211.2 0.3 fusion.41
  211.6 0.9 fusion.6
  (20 shorter events, 0.2 us)
Async XLA Ops:
  0.6 8.0 %copy-start = (bf16[1280,128]{1,0:T(8,128)(2,1)S(1)}, bf16[1280,128]{1,0:T(8,128)(2,1)}, u32[]{:S(2)}) copy-start(bf16[1280,128]{1,0:T(8,128)(2,1)} %param.20) | copy-start | bytes 983044
  136.5 2.5 %copy-start.1 = (bf16[2,4,128,1280]{3,2,1,0:T(8,128)(2,1)S(1)}, bf16[2,4,128,1280]{3,2,1,0:T(8,128)(2,1)}, u32[]{:S(2)}) copy-start(bf16[2,4,128,1280]{3,2,1,0:T(8,128)(2,1)} %get-tuple-element.6) | copy-start | bytes 7864324
  146.9 63.6 %copy-start.2 = (bf16[1,128,1280]{2,1,0:T(8,128)(2,1)S(1)}, bf16[1,128,1280]{2,1,0:T(8,128)(2,1)}, u32[]{:S(2)}) copy-start(bf16[1,128,1280]{2,1,0:T(8,128)(2,1)} %param.18) | copy-start | bytes 983044
  146.9 63.7 %copy-start.3 = (s32[1,128]{1,0:T(1,128)S(1)}, s32[1,128]{1,0:T(1,128)}, u32[]{:S(2)}) copy-start(s32[1,128]{1,0:T(1,128)} %param.23) | copy-start | bytes 1540

commit v3 on v2

--- a/solution.py
+++ b/solution.py
@@ -11,7 +11,8 @@
 
 MESH = pl.DeviceIdType.MESH
 norm_eps = 1e-06
-WIDTHS = (256, 256, 256, 256, 384)
+WIDTHS_IN = (256, 384, 384, 384)
+WIDTHS_OUT = (384, 384, 384, 256)
 SIDE = 128
 AWAY = (0, 3, 1, 2)
 CORES = 2
@@ -89,8 +90,7 @@
     return jnp.dot(table, values, preferred_element_type=jnp.float32).astype(jnp.bfloat16)
 
 
-def spans(model_width):
-    widths = WIDTHS
+def spans(model_width, widths):
     if sum(widths) != model_width + SIDE:
         widths = (model_width // 2, model_width - model_width // 2 + SIDE)
     return [(sum(widths[:t]), widths[t]) for t in range(len(widths))]
@@ -397,7 +397,7 @@
     rows = packed.shape[0]
     model_width, hidden = w_in.shape
     half_width = model_width // 2
-    spread = spans(model_width)
+    spread = spans(model_width, WIDTHS_IN)
     n = len(spread)
     yb, zb, cut = nz * CORES * SLOTS, ny * SLOTS, 4 * CORES * 2
     bf16, f32 = jnp.bfloat16, jnp.float32
@@ -460,7 +460,7 @@
         scratch_shapes=scratch,
         name="moe_fore",
         compiler_params=pltpu.CompilerParams(
-            collective_id=0, has_side_effects=True, vmem_limit_bytes=56 * 1024 * 1024
+            collective_id=0, has_side_effects=True, vmem_limit_bytes=46 * 1024 * 1024
         ),
     )(packed, u, w_in, w_out, perm, perm_small, perm_x)
 
@@ -599,7 +599,7 @@
     ny, nz = chip_sides(experts)
     rows = slope.shape[1]
     model_width, hidden = w_in.shape
-    spread = spans(model_width)
+    spread = spans(model_width, WIDTHS_OUT)
     n = len(spread)
     half = rows // 2
     bf16, f32 = jnp.bfloat16, jnp.float32
@@ -631,7 +631,7 @@
         scratch_shapes=scratch,
         name="moe_back",
         compiler_params=pltpu.CompilerParams(
-            collective_id=1, has_side_effects=True, vmem_limit_bytes=56 * 1024 * 1024
+            collective_id=1, has_side_effects=True, vmem_limit_bytes=40 * 1024 * 1024
         ),
     )(d_all, w_in, w_out, slope, hid, side, perm)
 
@@ -667,7 +667,11 @@
     packed = jnp.dot(
         slot_table, jnp.concatenate([normed_b, gate_side], 1), preferred_element_type=jnp.float32
     ).astype(jnp.bfloat16)
-    token_sums = jnp.sum(rows_in.reshape(2, seq_len, model_width), 1)
+    which = lax.broadcasted_iota(jnp.int32, (2, token_count), 1) // seq_len
+    members = (which == lax.broadcasted_iota(jnp.int32, (2, token_count), 0)).astype(jnp.bfloat16)
+    token_sums = jnp.dot(
+        members, tokens.reshape(token_count, model_width), preferred_element_type=jnp.float32
+    )
     everyone, slope, hid, side = fore_call(experts, seq_len, packed, token_sums, w_in[0], w_out[0])
     everyone = everyone.reshape(2, -1, model_width)
     pair_count = everyone.shape[1]

time: 213 us -> 205 us (0.962)
  Pallas kernels: 188 us -> 178 us
  local copies, waits for them, and re-layouts: 0.93 us -> 3.86 us
    pallas_call x1, Pallas kernels: 62.1 us -> 54 us  [back_call(): pl.pallas_call(functools.partial(back_kernel, ny, nz, spread), out_shape=...]
where the time goes in v3:
time: 205 us; the launch traced here: 204 us
  Pallas kernels  178 us (87%)
  other arithmetic  14.6 us (7%)
  matrix products  5.89 us (3%)
  local copies, waits for them, and re-layouts  3.86 us (2%)
    pallas_call x1, Pallas kernels, fore_call(): pl.pallas_call(functools.partial(fore_kernel, ny, nz, spread, 1.0 / seq_l...  124 us
    pallas_call x1, Pallas kernels, back_call(): pl.pallas_call(functools.partial(back_kernel, ny, nz, spread), out_shape=...  54 us

profile of v3, /device:TPU:1, one launch (start us, length us, event | category | flops | bytes accessed | tf_op | source)
XLA Modules:
  0.0 204.3 jit_solution(2422033961447349388)
XLA Ops:
  0.6 0.0 copy-start
  0.6 0.0 copy-start.7
  0.7 0.0 copy-start.5
  0.7 0.0 copy-start.8
  0.7 0.0 copy-start.1
  1.6 0.7 compare_bitcast_fusion
  2.2 0.7 add_bitcast_fusion
  2.9 1.1 convert_reduce_fusion
  4.0 1.2 fusion.9
  5.2 0.7 convert_element_type.69
  5.9 1.1 fusion.28.refs_1_
  7.0 1.2 fusion.11
  8.3 0.0 copy-done
  8.3 0.3 fusion.61
  8.6 0.7 select_reduce_fusion.1
  9.4 0.1 copy.20
  9.5 0.3 convolution_convert_fusion.refs_0_
  9.8 0.0 copy-done.7
  9.8 0.0 copy-done.5
  9.8 0.0 copy-done.8
  9.8 0.0 copy-done.1
  9.9 0.0 copy-start.2
  9.9 1.4 copy-done.2
  11.3 124.2 %moe_fore.1 = (bf16[2,4,128,1280]{3,2,1,0:T(8,128)(2,1)}, f32[4,256,640]{2,1,0:T(8,128)}, bf16[4,256,640]{2,1,0:T(8,128)(2,1)S(1)}, bf16[4,256,128]{2,1,0:T(8,128)(2,1)S(1)}) custom-call(bf16[256,1408]{1,0:T(8,128)(2,1)S(1)} %convolution_convert_fusion.refs_0_, f32[2,1280]{1,0:T(2,128)S(1)} %fusion.28.refs_1_, bf16[1280,640]{1,0:T(8,128)(2,1)S(1)} %bitcast.68, ...), custom_call_target="tpu_custom_call" | custom-call | tf_op jit(solution)/shard_map/moe_fore/pallas_call | solution.py:450
  135.5 0.0 copy-start.9
  135.5 2.5 %multiply_reduce_fusion = f32[2,4,128]{2,1,0:T(4,128)S(1)} fusion(bf16[2,4,128,1280]{3,2,1,0:T(8,128)(2,1)} %get-tuple-element.6), kind=kLoop, calls=%fused_computation.6 | loop fusion | flops 3931136 | bytes 2625536 | tf_op jit(solution)/shard_map/reduce_sum | solution.py:679
  138.0 0.0 copy-done.9
  138.1 0.2 fusion.60
  138.2 1.0 fusion.56
  139.2 0.4 exponential_reduce_fusion
  139.7 0.6 dynamic_slice.6
  140.3 1.1 fusion.15
  141.3 1.1 fusion.16
  142.5 0.8 fusion.1
  143.3 0.0 copy-start.3
  143.3 0.0 copy-start.4
  143.3 0.0 copy-start.6
  143.4 3.2 %fusion.58 = (bf16[2,512,1280]{2,1,0:T(8,128)(2,1)S(1)}, f32[2,512,1280]{2,1,0:T(8,128)}) fusion(f32[2,512]{1,0:T(2,128)S(1)} %broadcast_multiply_fusion, f32[2,512]{1,0:T(2,128)S(1)} %bitcast.84, f32[2,512]{1,0:T(2,128)S(1)} %bitcast.83, bf16[2,4,128,1280]{3,2,1,0:T(8,128)(2,1)S(1)} %copy-done.9, f32[1,512,1280]{2,1,0:T(8,128)S(1)} %bitcast.75, ...), kind=kLoop, calls=%fused_computation.109 | loop fusion | flops 9175040 | bytes 15740928 | tf_op jit(solution)/shard_map/convert_element_type | solution.py:711
  146.5 0.0 copy-done.3
  146.5 0.5 copy-done.4
  147.1 0.0 copy-done.6
  147.1 54.0 %moe_back.1 = bf16[256,1408]{1,0:T(8,128)(2,1)S(1)} custom-call(bf16[2,512,1280]{2,1,0:T(8,128)(2,1)S(1)} %get-tuple-element.17.refs_0_, bf16[1280,640]{1,0:T(8,128)(2,1)S(1)} %bitcast.69, bf16[640,1280]{1,0:T(8,128)(2,1)S(1)} %bitcast.71, f32[4,256,640]{2,1,0:T(8,128)S(1)} %copy-done.4, bf16[4,256,640]{2,1,0:T(8,128)(2,1)S(1)} %get-tuple-element.8.refs_4_, ...), custom_call_target="tpu_custom_call" | custom-call | tf_op jit(solution)/shard_map/moe_back/pallas_call | solution.py:626
  201.1 0.3 fusion.31
  201.4 0.1 slice_reduce_fusion
  201.6 0.6 fusion.12
  202.2 0.3 fusion.57
  202.5 0.9 constant_dynamic-slice_fusion
  203.4 0.9 fusion.14
  (23 shorter events, 0.1 us)
Async XLA Ops:
  0.6 7.6 %copy-start = (bf16[1280,128]{1,0:T(8,128)(2,1)S(1)}, bf16[1280,128]{1,0:T(8,128)(2,1)}, u32[]{:S(2)}) copy-start(bf16[1280,128]{1,0:T(8,128)(2,1)} %param.20) | copy-start | bytes 983044
  0.6 9.2 %copy-start.7 = (bf16[4,128,128]{2,1,0:T(8,128)(2,1)S(1)}, bf16[4,128,128]{2,1,0:T(8,128)(2,1)}, u32[]{:S(2)}) copy-start(bf16[4,128,128]{2,1,0:T(8,128)(2,1)} %constant.137.refs_6_) | copy-start | bytes 393220
  0.7 9.2 %copy-start.5 = (bf16[3,256,256]{2,1,0:T(8,128)(2,1)S(1)}, bf16[3,256,256]{2,1,0:T(8,128)(2,1)}, u32[]{:S(2)}) copy-start(bf16[3,256,256]{2,1,0:T(8,128)(2,1)} %constant.132.refs_4_) | copy-start | bytes 1179652
  0.7 9.2 %copy-start.8 = (bf16[128,128]{1,0:T(8,128)(2,1)S(1)}, bf16[128,128]{1,0:T(8,128)(2,1)}, u32[]{:S(2)}) copy-start(bf16[128,128]{1,0:T(8,128)(2,1)} %constant.118.clone.refs_5_) | copy-start | bytes 98308
  0.7 9.2 %copy-start.1 = (bf16[1,1280,640]{2,1,0:T(8,128)(2,1)S(1)}, bf16[1,1280,640]{2,1,0:T(8,128)(2,1)}, u32[]{:S(2)}) copy-start(bf16[1,1280,640]{2,1,0:T(8,128)(2,1)} %param.21) | copy-start | bytes 4915204
  9.9 1.4 copy-start.2
  135.5 2.5 %copy-start.9 = (bf16[2,4,128,1280]{3,2,1,0:T(8,128)(2,1)S(1)}, bf16[2,4,128,1280]{3,2,1,0:T(8,128)(2,1)}, u32[]{:S(2)}) copy-start(bf16[2,4,128,1280]{3,2,1,0:T(8,128)(2,1)} %get-tuple-element.6) | copy-start | bytes 7864324
  143.3 3.2 %copy-start.3 = (bf16[1,640,1280]{2,1,0:T(8,128)(2,1)S(1)}, bf16[1,640,1280]{2,1,0:T(8,128)(2,1)}, u32[]{:S(2)}) copy-start(bf16[1,640,1280]{2,1,0:T(8,128)(2,1)} %param.22) | copy-start | bytes 4915204
  143.3 3.7 %copy-start.4 = (f32[4,256,640]{2,1,0:T(8,128)S(1)}, f32[4,256,640]{2,1,0:T(8,128)}, u32[]{:S(2)}) copy-start(f32[4,256,640]{2,1,0:T(8,128)} %get-tuple-element.7.refs_3_) | copy-start | bytes 7864324
  143.3 3.8 %copy-start.6 = (bf16[256,256]{1,0:T(8,128)(2,1)S(1)}, bf16[256,256]{1,0:T(8,128)(2,1)}, u32[]{:S(2)}) copy-start(bf16[256,256]{1,0:T(8,128)(2,1)} %constant.116.clone.refs_6_) | copy-start | bytes 393220
  147.1 54.5 %copy-start.10 = (bf16[1,128,1280]{2,1,0:T(8,128)(2,1)S(1)}, bf16[1,128,1280]{2,1,0:T(8,128)(2,1)}, u32[]{:S(2)}) copy-start(bf16[1,128,1280]{2,1,0:T(8,128)(2,1)} %param.18) | copy-start | bytes 983044
  147.1 54.5 %copy-start.11 = (s32[1,128]{1,0:T(1,128)S(1)}, s32[1,128]{1,0:T(1,128)}, u32[]{:S(2)}) copy-start(s32[1,128]{1,0:T(1,128)} %param.23) | copy-start | bytes 1540

commit v4 on v3

--- a/solution.py
+++ b/solution.py
@@ -11,8 +11,8 @@
 
 MESH = pl.DeviceIdType.MESH
 norm_eps = 1e-06
-WIDTHS_IN = (256, 384, 384, 384)
-WIDTHS_OUT = (384, 384, 384, 256)
+WIDTHS_IN = (384, 512, 512)
+WIDTHS_OUT = (512, 512, 384)
 SIDE = 128
 AWAY = (0, 3, 1, 2)
 CORES = 2

time: 205 us -> 209 us (1.020)
  Pallas kernels: 178 us -> 181 us
    pallas_call x1, Pallas kernels: 124 us -> 127 us  [fore_call(): pl.pallas_call(functools.partial(fore_kernel, ny, nz, spread, 1.0 / seq_l...]
where the time goes in v4:
time: 209 us; the launch traced here: 207 us
  Pallas kernels  181 us (87%)
  other arithmetic  14.6 us (7%)
  matrix products  5.89 us (3%)
  local copies, waits for them, and re-layouts  3.86 us (2%)
    pallas_call x1, Pallas kernels, fore_call(): pl.pallas_call(functools.partial(fore_kernel, ny, nz, spread, 1.0 / seq_l...  127 us
    pallas_call x1, Pallas kernels, back_call(): pl.pallas_call(functools.partial(back_kernel, ny, nz, spread), out_shape=...  54.4 us

profile of v4, /device:TPU:1, one launch (start us, length us, event | category | flops | bytes accessed | tf_op | source)
XLA Modules:
  0.0 207.5 jit_solution(5483862865148628423)
XLA Ops:
  0.6 0.0 copy-start
  0.6 0.0 copy-start.7
  0.7 0.0 copy-start.5
  0.7 0.0 copy-start.8
  0.7 0.0 copy-start.1
  1.6 0.7 compare_bitcast_fusion
  2.2 0.7 add_bitcast_fusion
  2.9 1.1 convert_reduce_fusion
  4.0 1.2 fusion.9
  5.2 0.7 convert_element_type.69
  5.9 1.1 fusion.28.refs_1_
  7.0 1.2 fusion.11
  8.3 0.0 copy-done
  8.3 0.3 fusion.61
  8.6 0.7 select_reduce_fusion.1
  9.4 0.1 copy.20
  9.5 0.3 convolution_convert_fusion.refs_0_
  9.8 0.0 copy-done.7
  9.8 0.0 copy-done.5
  9.8 0.0 copy-done.8
  9.8 0.0 copy-done.1
  9.9 0.0 copy-start.2
  9.9 1.4 copy-done.2
  11.3 126.9 %moe_fore.1 = (bf16[2,4,128,1280]{3,2,1,0:T(8,128)(2,1)}, f32[4,256,640]{2,1,0:T(8,128)}, bf16[4,256,640]{2,1,0:T(8,128)(2,1)S(1)}, bf16[4,256,128]{2,1,0:T(8,128)(2,1)S(1)}) custom-call(bf16[256,1408]{1,0:T(8,128)(2,1)S(1)} %convolution_convert_fusion.refs_0_, f32[2,1280]{1,0:T(2,128)S(1)} %fusion.28.refs_1_, bf16[1280,640]{1,0:T(8,128)(2,1)S(1)} %bitcast.68, ...), custom_call_target="tpu_custom_call" | custom-call | tf_op jit(solution)/shard_map/moe_fore/pallas_call | solution.py:450
  138.2 0.0 copy-start.9
  138.3 2.5 %multiply_reduce_fusion = f32[2,4,128]{2,1,0:T(4,128)S(1)} fusion(bf16[2,4,128,1280]{3,2,1,0:T(8,128)(2,1)} %get-tuple-element.6), kind=kLoop, calls=%fused_computation.6 | loop fusion | flops 3931136 | bytes 2625536 | tf_op jit(solution)/shard_map/reduce_sum | solution.py:679
  140.8 0.0 copy-done.9
  140.8 0.2 fusion.60
  141.0 1.0 fusion.56
  142.0 0.4 exponential_reduce_fusion
  142.4 0.6 dynamic_slice.6
  143.0 1.1 fusion.15
  144.1 1.1 fusion.16
  145.2 0.8 fusion.1
  146.1 0.0 copy-start.3
  146.1 0.0 copy-start.4
  146.1 0.0 copy-start.6
  146.1 3.2 %fusion.58 = (bf16[2,512,1280]{2,1,0:T(8,128)(2,1)S(1)}, f32[2,512,1280]{2,1,0:T(8,128)}) fusion(f32[2,512]{1,0:T(2,128)S(1)} %broadcast_multiply_fusion, f32[2,512]{1,0:T(2,128)S(1)} %bitcast.84, f32[2,512]{1,0:T(2,128)S(1)} %bitcast.83, bf16[2,4,128,1280]{3,2,1,0:T(8,128)(2,1)S(1)} %copy-done.9, f32[1,512,1280]{2,1,0:T(8,128)S(1)} %bitcast.75, ...), kind=kLoop, calls=%fused_computation.109 | loop fusion | flops 9175040 | bytes 15740928 | tf_op jit(solution)/shard_map/convert_element_type | solution.py:711
  149.3 0.0 copy-done.3
  149.3 0.5 copy-done.4
  149.8 0.0 copy-done.6
  149.8 54.4 %moe_back.1 = bf16[256,1408]{1,0:T(8,128)(2,1)S(1)} custom-call(bf16[2,512,1280]{2,1,0:T(8,128)(2,1)S(1)} %get-tuple-element.17.refs_0_, bf16[1280,640]{1,0:T(8,128)(2,1)S(1)} %bitcast.69, bf16[640,1280]{1,0:T(8,128)(2,1)S(1)} %bitcast.71, f32[4,256,640]{2,1,0:T(8,128)S(1)} %copy-done.4, bf16[4,256,640]{2,1,0:T(8,128)(2,1)S(1)} %get-tuple-element.8.refs_4_, ...), custom_call_target="tpu_custom_call" | custom-call | tf_op jit(solution)/shard_map/moe_back/pallas_call | solution.py:626
  204.3 0.3 fusion.31
  204.6 0.1 slice_reduce_fusion
  204.7 0.6 fusion.12
  205.4 0.3 fusion.57
  205.7 0.9 constant_dynamic-slice_fusion
  206.6 0.9 fusion.14
  (23 shorter events, 0.1 us)
Async XLA Ops:
  0.6 7.6 %copy-start = (bf16[1280,128]{1,0:T(8,128)(2,1)S(1)}, bf16[1280,128]{1,0:T(8,128)(2,1)}, u32[]{:S(2)}) copy-start(bf16[1280,128]{1,0:T(8,128)(2,1)} %param.20) | copy-start | bytes 983044
  0.6 9.2 %copy-start.7 = (bf16[4,128,128]{2,1,0:T(8,128)(2,1)S(1)}, bf16[4,128,128]{2,1,0:T(8,128)(2,1)}, u32[]{:S(2)}) copy-start(bf16[4,128,128]{2,1,0:T(8,128)(2,1)} %constant.137.refs_6_) | copy-start | bytes 393220
  0.7 9.2 %copy-start.5 = (bf16[3,256,256]{2,1,0:T(8,128)(2,1)S(1)}, bf16[3,256,256]{2,1,0:T(8,128)(2,1)}, u32[]{:S(2)}) copy-start(bf16[3,256,256]{2,1,0:T(8,128)(2,1)} %constant.132.refs_4_) | copy-start | bytes 1179652
  0.7 9.2 %copy-start.8 = (bf16[128,128]{1,0:T(8,128)(2,1)S(1)}, bf16[128,128]{1,0:T(8,128)(2,1)}, u32[]{:S(2)}) copy-start(bf16[128,128]{1,0:T(8,128)(2,1)} %constant.118.clone.refs_5_) | copy-start | bytes 98308
  0.7 9.2 %copy-start.1 = (bf16[1,1280,640]{2,1,0:T(8,128)(2,1)S(1)}, bf16[1,1280,640]{2,1,0:T(8,128)(2,1)}, u32[]{:S(2)}) copy-start(bf16[1,1280,640]{2,1,0:T(8,128)(2,1)} %param.21) | copy-start | bytes 4915204
  9.9 1.4 copy-start.2
  138.2 2.5 %copy-start.9 = (bf16[2,4,128,1280]{3,2,1,0:T(8,128)(2,1)S(1)}, bf16[2,4,128,1280]{3,2,1,0:T(8,128)(2,1)}, u32[]{:S(2)}) copy-start(bf16[2,4,128,1280]{3,2,1,0:T(8,128)(2,1)} %get-tuple-element.6) | copy-start | bytes 7864324
  146.1 3.2 %copy-start.3 = (bf16[1,640,1280]{2,1,0:T(8,128)(2,1)S(1)}, bf16[1,640,1280]{2,1,0:T(8,128)(2,1)}, u32[]{:S(2)}) copy-start(bf16[1,640,1280]{2,1,0:T(8,128)(2,1)} %param.22) | copy-start | bytes 4915204
  146.1 3.7 %copy-start.4 = (f32[4,256,640]{2,1,0:T(8,128)S(1)}, f32[4,256,640]{2,1,0:T(8,128)}, u32[]{:S(2)}) copy-start(f32[4,256,640]{2,1,0:T(8,128)} %get-tuple-element.7.refs_3_) | copy-start | bytes 7864324
  146.1 3.8 %copy-start.6 = (bf16[256,256]{1,0:T(8,128)(2,1)S(1)}, bf16[256,256]{1,0:T(8,128)(2,1)}, u32[]{:S(2)}) copy-start(bf16[256,256]{1,0:T(8,128)(2,1)} %constant.116.clone.refs_6_) | copy-start | bytes 393220
  149.8 54.9 %copy-start.10 = (bf16[1,128,1280]{2,1,0:T(8,128)(2,1)S(1)}, bf16[1,128,1280]{2,1,0:T(8,128)(2,1)}, u32[]{:S(2)}) copy-start(bf16[1,128,1280]{2,1,0:T(8,128)(2,1)} %param.18) | copy-start | bytes 983044
  149.8 54.9 %copy-start.11 = (s32[1,128]{1,0:T(1,128)S(1)}, s32[1,128]{1,0:T(1,128)}, u32[]{:S(2)}) copy-start(s32[1,128]{1,0:T(1,128)} %param.23) | copy-start | bytes 1540
